TPU v7x, 768 devices: a whole 4x8x12 slice. The times are simulated.
768 devices in a mesh: leaf: 64 (over y, x, core), grp: 12 (over z).
Axes of the slice: x: 4, y: 8, z: 12, core: 2. Of those that a mesh axis runs over, the one named last changes fastest.
Arguments:
- moments: bfloat16 [786432, 256], P(('leaf', 'grp')), may hold values from -6 to 6
- live_fine: int32 [768], P(('leaf', 'grp')), may hold values from 64 to 1024, as said below
- near_requests: int32 [9216, 32], P(('leaf', 'grp')), may hold values from 0 to 1151, as said below
- far_requests: int32 [49152, 8], P(('leaf', 'grp')), may hold values from 1024 to 1167, as said below
- pair_source: int32 [12288, 1168], P(('leaf', 'grp')), may hold values from 0 to 2064, as said below
- child_up: bfloat16 [8, 256, 256], replicated, may hold values from -0.125 to 0.125
- child_down: bfloat16 [8, 256, 256], replicated, may hold values from -0.375 to 0.375
- offset_ops: bfloat16 [16, 256, 256], replicated, may hold values from -0.09375 to 0.09375
Outputs:
- expansions: bfloat16 [786432, 256], P(('leaf', 'grp'))
Inputs may be any that keep to these rules, and one draw needn't show every extreme that they name: `live_fine`: live cells of a device come first in its range; its middle and coarsest levels have ceil(n / 8) and ceil(n / 64) live cells. Some device has all 1024 live, some only 64. `near_requests`: A device's row g names, as indices into the cells of the device at position g of its group, 24 live finest-level cells and then 8 live middle-level cells. `far_requests`: A device's row l names, as indices into the cells of the device with leaf index l and the same grp index, 6 live middle-level cells and then 2 live coarsest cells. `pair_source`: A source row holds a cell of the target's level; cells that are not live take no source. Coarsest cells take sources from the leaf requests only.
All inputs are finite; a program needn't handle non-finite values.
Results may differ from a plain program's by a relative error of at most 0.01.
Values may be sent and summed in bfloat16 or wider, within the bound.
No kernel may reach another device: no remote copies, remote signals or barrier semaphores. Data moves between devices by JAX's collectives and lax.ppermute only.
A program may use at most 32 MiB of HBM per device.

v0:
```python
import jax
import jax.numpy as jnp
from jax import lax
from jax.sharding import PartitionSpec as P


def downward(parents, child_down):
    spread = jnp.einsum("cp,kpq->ckq", parents, child_down, preferred_element_type=jnp.float32)
    return spread.reshape(parents.shape[0] * 8, parents.shape[1])


def body(
    moments, live_fine, near_requests, far_requests, pair_source, child_up, child_down, offset_ops
):
    fine_count, coefficients = moments.shape
    middle_count = fine_count // 8
    coarse_count = fine_count // 64
    alive = jnp.arange(fine_count, dtype=jnp.int32)[:, None] < live_fine[0]
    fine_cells = jnp.where(alive, moments, jnp.zeros((), moments.dtype))
    upward = child_up.reshape(8 * coefficients, coefficients)
    middle = jnp.dot(
        fine_cells.reshape(middle_count, 8 * coefficients),
        upward,
        preferred_element_type=jnp.float32,
    ).astype(jnp.bfloat16)
    coarse = jnp.dot(
        middle.reshape(coarse_count, 8 * coefficients), upward, preferred_element_type=jnp.float32
    ).astype(jnp.bfloat16)
    all_cells = jnp.concatenate([fine_cells, middle, coarse], axis=0)
    replies = jnp.take(
        all_cells,
        lax.all_to_all(near_requests, "grp", split_axis=0, concat_axis=0, tiled=True),
        axis=0,
    )
    near_tiles = lax.all_to_all(replies, "grp", split_axis=0, concat_axis=0, tiled=True)
    replies = jnp.take(
        all_cells,
        lax.all_to_all(far_requests, "leaf", split_axis=0, concat_axis=0, tiled=True),
        axis=0,
    )
    far_tiles = lax.all_to_all(replies, "leaf", split_axis=0, concat_axis=0, tiled=True)
    empty_row = jnp.zeros((1, coefficients), jnp.bfloat16)
    sources = jnp.concatenate(
        [
            all_cells,
            near_tiles.reshape(-1, coefficients),
            far_tiles.reshape(-1, coefficients),
            empty_row,
        ],
        axis=0,
    )
    total_cells = all_cells.shape[0]

    def add_offset(total, inputs):
        rows, operator = inputs
        picked = jnp.take(sources, rows, axis=0)
        return (total + jnp.dot(picked, operator, preferred_element_type=jnp.float32), None)

    start = jnp.zeros((total_cells, coefficients), jnp.float32)
    far_field, unused = lax.scan(add_offset, start, (pair_source, offset_ops))
    coarse_local = far_field[fine_count + middle_count :].astype(jnp.bfloat16)
    middle_local = (
        far_field[fine_count : fine_count + middle_count] + downward(coarse_local, child_down)
    ).astype(jnp.bfloat16)
    expansion = far_field[:fine_count] + downward(middle_local, child_down)
    return jnp.where(alive, expansion, jnp.zeros((), expansion.dtype)).astype(jnp.bfloat16)


def solution(mesh):
    in_specs = (
        P(("leaf", "grp"), None),
        P(("leaf", "grp")),
        P(("leaf", "grp"), None),
        P(("leaf", "grp"), None),
        P(("leaf", "grp"), None),
        P(),
        P(),
        P(),
    )
    out_specs = P(("leaf", "grp"), None)
    return jax.shard_map(body, mesh=mesh, in_specs=in_specs, out_specs=out_specs, check_vma=False)
```

profile of v0, /device:TPU:1, one launch (start us, length us, event | category | flops | bytes accessed | tf_op | source)
XLA Modules:
  0.0 229.0 jit_solution(3893660293266914254)
XLA Ops:
  1.5 14.5 %all-to-all-start.2 = ((s32[64,1,8]{2,1,0:T(1,128)}), s32[64,1,8]{2,1,0:T(1,128)S(1)}, u32[]{:S(2)}, u32[]{:S(2)}) async-start(s32[64,1,8]{2,1,0:T(1,128)} %bitcast.5), calls=%async_computation.2 | async-start | bytes 65536 | tf_op jit(solution)/shard_map/all_to_all | solution.py:38
  19.9 5.6 %all-to-all-done.2 = s32[64,1,8]{2,1,0:T(1,128)S(1)} async-done(((s32[64,1,8]{2,1,0:T(1,128)}), s32[64,1,8]{2,1,0:T(1,128)S(1)}, u32[]{:S(2)}, u32[]{:S(2)}) %all-to-all-start.2) | async-done | bytes 2080 | tf_op jit(solution)/shard_map/all_to_all | solution.py:38
  25.4 11.8 %all-to-all-start = ((s32[12,1,32]{2,1,0:T(1,128)}), s32[12,1,32]{2,1,0:T(1,128)S(1)}, u32[]{:S(2)}, u32[]{:S(2)}) async-start(s32[12,1,32]{2,1,0:T(1,128)} %all_to_all.26), calls=%async_computation | async-start | bytes 12288 | tf_op jit(solution)/shard_map/all_to_all | solution.py:32
  37.4 8.9 %all-to-all-done = s32[12,1,32]{2,1,0:T(1,128)S(1)} async-done(((s32[12,1,32]{2,1,0:T(1,128)}), s32[12,1,32]{2,1,0:T(1,128)S(1)}, u32[]{:S(2)}, u32[]{:S(2)}) %all-to-all-start) | async-done | bytes 1568 | tf_op jit(solution)/shard_map/all_to_all | solution.py:32
  49.2 3.5 %all-to-all-start.1 = ((bf16[12,32,256]{2,1,0:T(8,128)(2,1)}), bf16[12,32,256]{2,1,0:T(8,128)(2,1)S(1)}, u32[]{:S(2)}, u32[]{:S(2)}) async-start(bf16[12,32,256]{2,1,0:T(8,128)(2,1)} %broadcast_select_fusion.1), calls=%async_computation.1 | async-start | bytes 393216 | tf_op jit(solution)/shard_map/all_to_all | solution.py:35
  55.6 8.7 %all-to-all-done.1 = bf16[12,32,256]{2,1,0:T(8,128)(2,1)S(1)} async-done(((bf16[12,32,256]{2,1,0:T(8,128)(2,1)}), bf16[12,32,256]{2,1,0:T(8,128)(2,1)S(1)}, u32[]{:S(2)}, u32[]{:S(2)}) %all-to-all-start.1) | async-done | bytes 196640 | tf_op jit(solution)/shard_map/all_to_all | solution.py:35
  64.3 8.8 %all-to-all-start.3 = ((bf16[64,8,256]{2,1,0:T(8,128)(2,1)}), bf16[64,8,256]{2,1,0:T(8,128)(2,1)S(1)}, u32[]{:S(2)}, u32[]{:S(2)}) async-start(bf16[64,8,256]{2,1,0:T(8,128)(2,1)} %bitcast_select_fusion), calls=%async_computation.3 | async-start | bytes 524288 | tf_op jit(solution)/shard_map/all_to_all | solution.py:41
  73.1 13.1 %all-to-all-done.3 = bf16[64,8,256]{2,1,0:T(8,128)(2,1)S(1)} async-done(((bf16[64,8,256]{2,1,0:T(8,128)(2,1)}), bf16[64,8,256]{2,1,0:T(8,128)(2,1)S(1)}, u32[]{:S(2)}, u32[]{:S(2)}) %all-to-all-start.3) | async-done | bytes 262176 | tf_op jit(solution)/shard_map/all_to_all | solution.py:41
  86.3 138.0 %while.11 = (s32[]{:T(128)}, f32[1168,256]{1,0:T(8,128)}, s32[16,1168]{1,0:T(8,128)}, bf16[2065,256]{1,0:T(8,128)(2,1)S(1)}, bf16[16,256,256]{2,1,0:T(8,128)(2,1)}, /*index=5*/s32[]{:T(128)}, s32[]{:T(128)}) while((s32[]{:T(128)}, f32[1168,256]{1,0:T(8,128)}, s32[16,1168]{1,0:T(8,128)}, bf16[2065,256]{1,0:T(8,128)(2,1)S(1)}, ...), condition=%wide.region_1.2_spmd.clone, body=%wide.region_0.1_spmd.clone.sunk | while | flops 154001680 | bytes 4361023 | solution.py:60
  87.1 4.2 %gather_fusion = bf16[1168,256]{1,0:T(8,128)(2,1)S(1)} fusion(bf16[2065,256]{1,0:T(8,128)(2,1)S(1)} %get-tuple-element.117, s32[2048]{0:T(1024)S(1)} %pad_clamp_fusion.4), kind=kCustom, calls=%fused_computation.clone.clone.1 | custom fusion | bytes 1200704 | tf_op jit(solution)/shard_map/while/body/eval_jaxpr/jit(_take)/gather | solution.py:56
  95.3 4.2 %gather_fusion = bf16[1168,256]{1,0:T(8,128)(2,1)S(1)} fusion(bf16[2065,256]{1,0:T(8,128)(2,1)S(1)} %get-tuple-element.117, s32[2048]{0:T(1024)S(1)} %pad_clamp_fusion.4), kind=kCustom, calls=%fused_computation.clone.clone.1 | custom fusion | bytes 1200704 | tf_op jit(solution)/shard_map/while/body/eval_jaxpr/jit(_take)/gather | solution.py:56
  100.4 2.8 %convolution_add_fusion.2 = f32[1168,256]{1,0:T(8,128)} fusion(f32[1168,256]{1,0:T(8,128)} %get-tuple-element.108, bf16[1168,256]{1,0:T(8,128)(2,1)S(1)} %gather_fusion, pred[1168]{0:T(1024)(128)(4,1)S(1)} %compare_and_fusion.4, pred[]{:T(512)S(6)} %compare.3, bf16[16,256,256]{2,1,0:T(8,128)(2,1)} %get-tuple-element.118, s32[]{:T(128)} %get-tuple-element.107), kind=kOutput, calls=%fused_computation.3.clone.1 | convolution fusion | flops 153989120 | bytes 3122833 | tf_op jit(solution)/shard_map/while/body/eval_jaxpr/dot_general | solution.py:57
  104.0 4.2 %gather_fusion = bf16[1168,256]{1,0:T(8,128)(2,1)S(1)} fusion(bf16[2065,256]{1,0:T(8,128)(2,1)S(1)} %get-tuple-element.117, s32[2048]{0:T(1024)S(1)} %pad_clamp_fusion.4), kind=kCustom, calls=%fused_computation.clone.clone.1 | custom fusion | bytes 1200704 | tf_op jit(solution)/shard_map/while/body/eval_jaxpr/jit(_take)/gather | solution.py:56
  109.0 2.8 %convolution_add_fusion.2 = f32[1168,256]{1,0:T(8,128)} fusion(f32[1168,256]{1,0:T(8,128)} %get-tuple-element.108, bf16[1168,256]{1,0:T(8,128)(2,1)S(1)} %gather_fusion, pred[1168]{0:T(1024)(128)(4,1)S(1)} %compare_and_fusion.4, pred[]{:T(512)S(6)} %compare.3, bf16[16,256,256]{2,1,0:T(8,128)(2,1)} %get-tuple-element.118, s32[]{:T(128)} %get-tuple-element.107), kind=kOutput, calls=%fused_computation.3.clone.1 | convolution fusion | flops 153989120 | bytes 3122833 | tf_op jit(solution)/shard_map/while/body/eval_jaxpr/dot_general | solution.py:57
  112.6 4.2 %gather_fusion = bf16[1168,256]{1,0:T(8,128)(2,1)S(1)} fusion(bf16[2065,256]{1,0:T(8,128)(2,1)S(1)} %get-tuple-element.117, s32[2048]{0:T(1024)S(1)} %pad_clamp_fusion.4), kind=kCustom, calls=%fused_computation.clone.clone.1 | custom fusion | bytes 1200704 | tf_op jit(solution)/shard_map/while/body/eval_jaxpr/jit(_take)/gather | solution.py:56
  121.3 4.2 %gather_fusion = bf16[1168,256]{1,0:T(8,128)(2,1)S(1)} fusion(bf16[2065,256]{1,0:T(8,128)(2,1)S(1)} %get-tuple-element.117, s32[2048]{0:T(1024)S(1)} %pad_clamp_fusion.4), kind=kCustom, calls=%fused_computation.clone.clone.1 | custom fusion | bytes 1200704 | tf_op jit(solution)/shard_map/while/body/eval_jaxpr/jit(_take)/gather | solution.py:56
  126.3 2.8 %convolution_add_fusion.2 = f32[1168,256]{1,0:T(8,128)} fusion(f32[1168,256]{1,0:T(8,128)} %get-tuple-element.108, bf16[1168,256]{1,0:T(8,128)(2,1)S(1)} %gather_fusion, pred[1168]{0:T(1024)(128)(4,1)S(1)} %compare_and_fusion.4, pred[]{:T(512)S(6)} %compare.3, bf16[16,256,256]{2,1,0:T(8,128)(2,1)} %get-tuple-element.118, s32[]{:T(128)} %get-tuple-element.107), kind=kOutput, calls=%fused_computation.3.clone.1 | convolution fusion | flops 153989120 | bytes 3122833 | tf_op jit(solution)/shard_map/while/body/eval_jaxpr/dot_general | solution.py:57
  129.9 4.2 %gather_fusion = bf16[1168,256]{1,0:T(8,128)(2,1)S(1)} fusion(bf16[2065,256]{1,0:T(8,128)(2,1)S(1)} %get-tuple-element.117, s32[2048]{0:T(1024)S(1)} %pad_clamp_fusion.4), kind=kCustom, calls=%fused_computation.clone.clone.1 | custom fusion | bytes 1200704 | tf_op jit(solution)/shard_map/while/body/eval_jaxpr/jit(_take)/gather | solution.py:56
  138.6 4.2 %gather_fusion = bf16[1168,256]{1,0:T(8,128)(2,1)S(1)} fusion(bf16[2065,256]{1,0:T(8,128)(2,1)S(1)} %get-tuple-element.117, s32[2048]{0:T(1024)S(1)} %pad_clamp_fusion.4), kind=kCustom, calls=%fused_computation.clone.clone.1 | custom fusion | bytes 1200704 | tf_op jit(solution)/shard_map/while/body/eval_jaxpr/jit(_take)/gather | solution.py:56
  147.2 4.2 %gather_fusion = bf16[1168,256]{1,0:T(8,128)(2,1)S(1)} fusion(bf16[2065,256]{1,0:T(8,128)(2,1)S(1)} %get-tuple-element.117, s32[2048]{0:T(1024)S(1)} %pad_clamp_fusion.4), kind=kCustom, calls=%fused_computation.clone.clone.1 | custom fusion | bytes 1200704 | tf_op jit(solution)/shard_map/while/body/eval_jaxpr/jit(_take)/gather | solution.py:56
  152.3 2.8 %convolution_add_fusion.2 = f32[1168,256]{1,0:T(8,128)} fusion(f32[1168,256]{1,0:T(8,128)} %get-tuple-element.108, bf16[1168,256]{1,0:T(8,128)(2,1)S(1)} %gather_fusion, pred[1168]{0:T(1024)(128)(4,1)S(1)} %compare_and_fusion.4, pred[]{:T(512)S(6)} %compare.3, bf16[16,256,256]{2,1,0:T(8,128)(2,1)} %get-tuple-element.118, s32[]{:T(128)} %get-tuple-element.107), kind=kOutput, calls=%fused_computation.3.clone.1 | convolution fusion | flops 153989120 | bytes 3122833 | tf_op jit(solution)/shard_map/while/body/eval_jaxpr/dot_general | solution.py:57
  155.9 4.2 %gather_fusion = bf16[1168,256]{1,0:T(8,128)(2,1)S(1)} fusion(bf16[2065,256]{1,0:T(8,128)(2,1)S(1)} %get-tuple-element.117, s32[2048]{0:T(1024)S(1)} %pad_clamp_fusion.4), kind=kCustom, calls=%fused_computation.clone.clone.1 | custom fusion | bytes 1200704 | tf_op jit(solution)/shard_map/while/body/eval_jaxpr/jit(_take)/gather | solution.py:56
  164.5 4.2 %gather_fusion = bf16[1168,256]{1,0:T(8,128)(2,1)S(1)} fusion(bf16[2065,256]{1,0:T(8,128)(2,1)S(1)} %get-tuple-element.117, s32[2048]{0:T(1024)S(1)} %pad_clamp_fusion.4), kind=kCustom, calls=%fused_computation.clone.clone.1 | custom fusion | bytes 1200704 | tf_op jit(solution)/shard_map/while/body/eval_jaxpr/jit(_take)/gather | solution.py:56
  169.6 2.8 %convolution_add_fusion.2 = f32[1168,256]{1,0:T(8,128)} fusion(f32[1168,256]{1,0:T(8,128)} %get-tuple-element.108, bf16[1168,256]{1,0:T(8,128)(2,1)S(1)} %gather_fusion, pred[1168]{0:T(1024)(128)(4,1)S(1)} %compare_and_fusion.4, pred[]{:T(512)S(6)} %compare.3, bf16[16,256,256]{2,1,0:T(8,128)(2,1)} %get-tuple-element.118, s32[]{:T(128)} %get-tuple-element.107), kind=kOutput, calls=%fused_computation.3.clone.1 | convolution fusion | flops 153989120 | bytes 3122833 | tf_op jit(solution)/shard_map/while/body/eval_jaxpr/dot_general | solution.py:57
  173.2 4.2 %gather_fusion = bf16[1168,256]{1,0:T(8,128)(2,1)S(1)} fusion(bf16[2065,256]{1,0:T(8,128)(2,1)S(1)} %get-tuple-element.117, s32[2048]{0:T(1024)S(1)} %pad_clamp_fusion.4), kind=kCustom, calls=%fused_computation.clone.clone.1 | custom fusion | bytes 1200704 | tf_op jit(solution)/shard_map/while/body/eval_jaxpr/jit(_take)/gather | solution.py:56
  178.2 2.8 %convolution_add_fusion.2 = f32[1168,256]{1,0:T(8,128)} fusion(f32[1168,256]{1,0:T(8,128)} %get-tuple-element.108, bf16[1168,256]{1,0:T(8,128)(2,1)S(1)} %gather_fusion, pred[1168]{0:T(1024)(128)(4,1)S(1)} %compare_and_fusion.4, pred[]{:T(512)S(6)} %compare.3, bf16[16,256,256]{2,1,0:T(8,128)(2,1)} %get-tuple-element.118, s32[]{:T(128)} %get-tuple-element.107), kind=kOutput, calls=%fused_computation.3.clone.1 | convolution fusion | flops 153989120 | bytes 3122833 | tf_op jit(solution)/shard_map/while/body/eval_jaxpr/dot_general | solution.py:57
  181.8 4.2 %gather_fusion = bf16[1168,256]{1,0:T(8,128)(2,1)S(1)} fusion(bf16[2065,256]{1,0:T(8,128)(2,1)S(1)} %get-tuple-element.117, s32[2048]{0:T(1024)S(1)} %pad_clamp_fusion.4), kind=kCustom, calls=%fused_computation.clone.clone.1 | custom fusion | bytes 1200704 | tf_op jit(solution)/shard_map/while/body/eval_jaxpr/jit(_take)/gather | solution.py:56
  190.5 4.2 %gather_fusion = bf16[1168,256]{1,0:T(8,128)(2,1)S(1)} fusion(bf16[2065,256]{1,0:T(8,128)(2,1)S(1)} %get-tuple-element.117, s32[2048]{0:T(1024)S(1)} %pad_clamp_fusion.4), kind=kCustom, calls=%fused_computation.clone.clone.1 | custom fusion | bytes 1200704 | tf_op jit(solution)/shard_map/while/body/eval_jaxpr/jit(_take)/gather | solution.py:56
  199.2 4.2 %gather_fusion = bf16[1168,256]{1,0:T(8,128)(2,1)S(1)} fusion(bf16[2065,256]{1,0:T(8,128)(2,1)S(1)} %get-tuple-element.117, s32[2048]{0:T(1024)S(1)} %pad_clamp_fusion.4), kind=kCustom, calls=%fused_computation.clone.clone.1 | custom fusion | bytes 1200704 | tf_op jit(solution)/shard_map/while/body/eval_jaxpr/jit(_take)/gather | solution.py:56
  204.2 2.8 %convolution_add_fusion.2 = f32[1168,256]{1,0:T(8,128)} fusion(f32[1168,256]{1,0:T(8,128)} %get-tuple-element.108, bf16[1168,256]{1,0:T(8,128)(2,1)S(1)} %gather_fusion, pred[1168]{0:T(1024)(128)(4,1)S(1)} %compare_and_fusion.4, pred[]{:T(512)S(6)} %compare.3, bf16[16,256,256]{2,1,0:T(8,128)(2,1)} %get-tuple-element.118, s32[]{:T(128)} %get-tuple-element.107), kind=kOutput, calls=%fused_computation.3.clone.1 | convolution fusion | flops 153989120 | bytes 3122833 | tf_op jit(solution)/shard_map/while/body/eval_jaxpr/dot_general | solution.py:57
  207.8 4.2 %gather_fusion = bf16[1168,256]{1,0:T(8,128)(2,1)S(1)} fusion(bf16[2065,256]{1,0:T(8,128)(2,1)S(1)} %get-tuple-element.117, s32[2048]{0:T(1024)S(1)} %pad_clamp_fusion.4), kind=kCustom, calls=%fused_computation.clone.clone.1 | custom fusion | bytes 1200704 | tf_op jit(solution)/shard_map/while/body/eval_jaxpr/jit(_take)/gather | solution.py:56
  216.5 4.2 %gather_fusion = bf16[1168,256]{1,0:T(8,128)(2,1)S(1)} fusion(bf16[2065,256]{1,0:T(8,128)(2,1)S(1)} %get-tuple-element.117, s32[2048]{0:T(1024)S(1)} %pad_clamp_fusion.4), kind=kCustom, calls=%fused_computation.clone.clone.1 | custom fusion | bytes 1200704 | tf_op jit(solution)/shard_map/while/body/eval_jaxpr/jit(_take)/gather | solution.py:56
  (106 shorter events, 65.8 us)
Async XLA Ops:
  0.0 18.2 %copy-start = (bf16[8,256,256]{2,1,0:T(8,128)(2,1)S(1)}, bf16[8,256,256]{2,1,0:T(8,128)(2,1)}, u32[]{:S(2)}) copy-start(bf16[8,256,256]{2,1,0:T(8,128)(2,1)} %param.15) | copy-start | bytes 3145732
  1.5 24.0 %all-to-all-start.2 = ((s32[64,1,8]{2,1,0:T(1,128)}), s32[64,1,8]{2,1,0:T(1,128)S(1)}, u32[]{:S(2)}, u32[]{:S(2)}) async-start(s32[64,1,8]{2,1,0:T(1,128)} %bitcast.5), calls=%async_computation.2 | async-start | bytes 65536 | tf_op jit(solution)/shard_map/all_to_all | solution.py:38
  18.6 0.7 copy-start.2
  25.4 20.8 %all-to-all-start = ((s32[12,1,32]{2,1,0:T(1,128)}), s32[12,1,32]{2,1,0:T(1,128)S(1)}, u32[]{:S(2)}, u32[]{:S(2)}) async-start(s32[12,1,32]{2,1,0:T(1,128)} %all_to_all.26), calls=%async_computation | async-start | bytes 12288 | tf_op jit(solution)/shard_map/all_to_all | solution.py:32
  49.2 15.1 %all-to-all-start.1 = ((bf16[12,32,256]{2,1,0:T(8,128)(2,1)}), bf16[12,32,256]{2,1,0:T(8,128)(2,1)S(1)}, u32[]{:S(2)}, u32[]{:S(2)}) async-start(bf16[12,32,256]{2,1,0:T(8,128)(2,1)} %broadcast_select_fusion.1), calls=%async_computation.1 | async-start | bytes 393216 | tf_op jit(solution)/shard_map/all_to_all | solution.py:35
  64.3 21.9 %all-to-all-start.3 = ((bf16[64,8,256]{2,1,0:T(8,128)(2,1)}), bf16[64,8,256]{2,1,0:T(8,128)(2,1)S(1)}, u32[]{:S(2)}, u32[]{:S(2)}) async-start(bf16[64,8,256]{2,1,0:T(8,128)(2,1)} %bitcast_select_fusion), calls=%async_computation.3 | async-start | bytes 524288 | tf_op jit(solution)/shard_map/all_to_all | solution.py:41
  224.3 1.6 copy-start.1
where the time goes:
time: 232 us; the launch traced here: 229 us
  local copies, waits for them, and re-layouts  87.3 us (38%)
  matrix products  47.8 us (21%)
  starting transfers between devices  38.7 us (17%)
  waiting for transfers between devices  36.3 us (16%)
  other arithmetic  17.6 us (8%)
    gather x16, local copies, waits for them, and re-layouts, add_offset(): picked = jnp.take(sources, rows, axis=0)  67.4 us
    dot_general x16, matrix products, add_offset(): jnp.dot(picked, operator, preferred_element_type=jnp.float32)  44.1 us
    all_to_all x1, starting transfers between devices, body(): lax.all_to_all(far_requests, 'leaf', split_axis=0, concat_axis=0, tiled=T...  14.5 us
    all_to_all x1, waiting for transfers between devices, body(): lax.all_to_all(replies, 'leaf', split_axis=0, concat_axis=0, tiled=True)  13.1 us
    dynamic_slice x16, local copies, waits for them, and re-layouts, body(): far_field, unused = lax.scan(add_offset, start, (pair_source, offset_ops))  12.9 us
    select_n x16, other arithmetic, add_offset(): picked = jnp.take(sources, rows, axis=0)  12.9 us
    all_to_all x1, starting transfers between devices, body(): lax.all_to_all(near_requests, 'grp', split_axis=0, concat_axis=0, tiled=T...  11.8 us
    all_to_all x1, waiting for transfers between devices, body(): lax.all_to_all(near_requests, 'grp', split_axis=0, concat_axis=0, tiled=T...  8.86 us
  transfers between devices with their start and end apart: 4, of which 4 were waited for; matrix products, arithmetic and copies ran while one was open for 2% of the time, Pallas kernels for 0%

commit v1 on v0

v1 whole, which is shorter than its diff:
```python
import functools

import jax
import jax.numpy as jnp
from jax import lax
from jax.experimental import pallas as pl
from jax.experimental.pallas import tpu as pltpu
from jax.sharding import PartitionSpec as P

BF16 = jnp.bfloat16
F32 = jnp.float32
TILE = 256
VMEM = pl.BlockSpec(memory_space=pltpu.VMEM)


def one_hot(column, base, width):
    rows = column.shape[0]
    wide = jnp.broadcast_to(column - base, (rows, 128)).astype(jnp.int16)
    lane = lax.broadcasted_iota(jnp.int32, (rows, 128), 1).astype(jnp.int16)
    one = jnp.ones((rows, 128), BF16)
    zero = jnp.zeros((rows, 128), BF16)
    parts = [jnp.where(wide == lane + jnp.int16(128 * k), one, zero) for k in range(width // 128)]
    return parts[0] if len(parts) == 1 else jnp.concatenate(parts, axis=1)


def dot(a, b):
    return jnp.dot(a, b, preferred_element_type=F32)


def own_kernel(first, offsets, fine_ref, pairs_ref, ops_ref, *refs):
    if first:
        out_ref, moved_ref = refs
    else:
        in_ref, out_ref, moved_ref = refs
    count = fine_ref.shape[0]
    for n, o in enumerate(offsets):
        moved_ref[n % 2] = dot(fine_ref[...], ops_ref[o]).astype(BF16)
        for m in range(count // TILE):
            rows = slice(m * TILE, (m + 1) * TILE)
            part = dot(one_hot(pairs_ref[rows, o : o + 1], 0, count), moved_ref[n % 2])
            if n > 0:
                part = part + out_ref[rows, :]
            elif not first:
                part = part + in_ref[rows, :]
            out_ref[rows, :] = part


def own_pass(fine, pairs, ops, offsets, total):
    count, size = fine.shape
    first = total is None
    args = (fine, pairs, ops) if first else (fine, pairs, ops, total)
    macs = len(offsets) * count * size * (size + count)
    return pl.pallas_call(
        functools.partial(own_kernel, first, offsets),
        out_shape=jax.ShapeDtypeStruct((count, size), F32),
        in_specs=[VMEM] * len(args),
        out_specs=VMEM,
        scratch_shapes=[pltpu.VMEM((2, count, size), BF16)],
        compiler_params=pltpu.CompilerParams(vmem_limit_bytes=24 << 20),
        cost_estimate=pl.CostEstimate(flops=2 * macs, bytes_accessed=4 << 20, transcendentals=0),
        name="own_pass",
    )(*args)


def near_kernel(near_base, near_ref, mid_ref, pairs_ref, ops_ref, total_ref, out_ref, out_mid_ref, moved_ref, picked_ref):
    count = total_ref.shape[0]
    middles = mid_ref.shape[0]
    near = near_ref.shape[0]
    offsets = ops_ref.shape[0]
    for o in range(offsets):
        moved_ref[o % 2] = dot(near_ref[...], ops_ref[o]).astype(BF16)
        for m in range(count // TILE):
            rows = slice(m * TILE, (m + 1) * TILE)
            part = dot(one_hot(pairs_ref[rows, o : o + 1], near_base, near), moved_ref[o % 2])
            if o > 0:
                part = part + out_ref[rows, :]
            else:
                part = part + total_ref[rows, :]
            out_ref[rows, :] = part
    for o in range(offsets):
        column = pairs_ref[count : count + middles, o : o + 1]
        part = dot(one_hot(column, count, middles), mid_ref[...])
        part = part + dot(one_hot(column, near_base, near), near_ref[...])
        picked_ref[o] = part.astype(BF16)
    mid = dot(picked_ref[0], ops_ref[0])
    for o in range(1, offsets):
        mid = mid + dot(picked_ref[o], ops_ref[o])
    out_mid_ref[...] = mid


def near_pass(near_base, near, mid, pairs, ops, total):
    count, size = total.shape
    offsets = ops.shape[0]
    macs = offsets * near.shape[0] * size * (size + count)
    return pl.pallas_call(
        functools.partial(near_kernel, near_base),
        out_shape=(
            jax.ShapeDtypeStruct((count, size), F32),
            jax.ShapeDtypeStruct(mid.shape, F32),
        ),
        in_specs=[VMEM] * 5,
        out_specs=(VMEM, VMEM),
        scratch_shapes=[
            pltpu.VMEM((2,) + near.shape, BF16),
            pltpu.VMEM((offsets,) + mid.shape, BF16),
        ],
        compiler_params=pltpu.CompilerParams(vmem_limit_bytes=24 << 20),
        cost_estimate=pl.CostEstimate(flops=2 * macs, bytes_accessed=6 << 20, transcendentals=0),
        name="near_pass",
    )(near, mid, pairs, ops, total)


def far_kernel(far_base, live_ref, far_ref, pairs_ref, ops_ref, down_ref, mid_ref, total_ref, out_ref, picked_ref, mid_wide, fine_wide):
    count = total_ref.shape[0]
    middles = mid_ref.shape[0]
    cells = pairs_ref.shape[0]
    far = far_ref.shape[0]
    offsets = ops_ref.shape[0]
    for o in range(offsets):
        column = pairs_ref[:, o : o + 1]
        picked_ref[o] = dot(one_hot(column, far_base, far), far_ref[...]).astype(BF16)
    field = dot(picked_ref[0], ops_ref[0])
    for o in range(1, offsets):
        field = field + dot(picked_ref[o], ops_ref[o])
    coarse = field[middles:, :].astype(BF16)
    coarses = cells - middles
    for k in range(8):
        rows = pl.ds(k, coarses, stride=8)
        spread = dot(coarse, down_ref[k])
        mid_wide[0, rows, :] = spread[:, :128]
        mid_wide[1, rows, :] = spread[:, 128:]
    spread = jnp.concatenate([mid_wide[0], mid_wide[1]], axis=1)
    mid = (field[:middles, :] + mid_ref[...] + spread).astype(BF16)
    for k in range(8):
        rows = pl.ds(k, middles, stride=8)
        spread = dot(mid, down_ref[k])
        fine_wide[0, rows, :] = spread[:, :128]
        fine_wide[1, rows, :] = spread[:, 128:]
    live = live_ref[0]
    for m in range(count // TILE):
        rows = slice(m * TILE, (m + 1) * TILE)
        row = lax.broadcasted_iota(jnp.int32, (TILE, 1), 0) + m * TILE
        spread = jnp.concatenate([fine_wide[0, rows, :], fine_wide[1, rows, :]], axis=1)
        out_ref[rows, :] = jnp.where(row < live, total_ref[rows, :] + spread, 0.0).astype(BF16)


def far_pass(far_base, live, far, pairs, ops, down, mid, total):
    count, size = total.shape
    offsets = ops.shape[0]
    cells = pairs.shape[0]
    macs = offsets * cells * size * (far.shape[0] + size) + count * size * size
    return pl.pallas_call(
        functools.partial(far_kernel, far_base),
        out_shape=jax.ShapeDtypeStruct((count, size), BF16),
        in_specs=[pl.BlockSpec(memory_space=pltpu.SMEM)] + [VMEM] * 6,
        out_specs=VMEM,
        scratch_shapes=[
            pltpu.VMEM((offsets, cells, size), BF16),
            pltpu.VMEM((2, mid.shape[0], 128), F32),
            pltpu.VMEM((2, count, 128), F32),
        ],
        compiler_params=pltpu.CompilerParams(vmem_limit_bytes=24 << 20),
        cost_estimate=pl.CostEstimate(flops=2 * macs, bytes_accessed=6 << 20, transcendentals=0),
        name="far_pass",
    )(live, far, pairs, ops, down, mid, total)


def exchange(rows, axis):
    return lax.all_to_all(rows, axis, split_axis=0, concat_axis=0, tiled=True)


def pick(table, index):
    rows = jnp.take(table, index.reshape(-1), axis=0, mode="clip")
    return rows.reshape(index.shape + table.shape[1:])


def body(
    moments, live_fine, near_requests, far_requests, pair_source, child_up, child_down, offset_ops
):
    fine_count, size = moments.shape
    middle_count = fine_count // 8
    coarse_count = fine_count // 64
    cells = fine_count + middle_count + coarse_count
    offsets = offset_ops.shape[0]
    near_asked = exchange(near_requests, "grp")
    far_asked = exchange(far_requests, "leaf")
    alive = jnp.arange(fine_count, dtype=jnp.int32)[:, None] < live_fine[0]
    fine = jnp.where(alive, moments, jnp.zeros((), moments.dtype))
    upward = child_up.reshape(8 * size, size)
    middle = dot(fine.reshape(middle_count, 8 * size), upward).astype(BF16)
    coarse = dot(middle.reshape(coarse_count, 8 * size), upward).astype(BF16)
    pairs = pair_source.T
    near_tiles = exchange(pick(jnp.concatenate([fine, middle]), near_asked), "grp")
    far_tiles = exchange(pick(jnp.concatenate([middle, coarse]), far_asked - fine_count), "leaf")
    near_tiles = near_tiles.reshape(-1, size)
    far_tiles = far_tiles.reshape(-1, size)
    half = offsets // 2
    total = own_pass(fine, pairs, offset_ops, tuple(range(half)), None)
    total = own_pass(fine, pairs, offset_ops, tuple(range(half, offsets)), total)
    total, mid = near_pass(cells, near_tiles, middle, pairs, offset_ops, total)
    far_base = cells + near_tiles.shape[0]
    return far_pass(
        far_base, live_fine, far_tiles, pairs[fine_count:], offset_ops, child_down, mid, total
    )


def solution(mesh):
    in_specs = (
        P(("leaf", "grp"), None),
        P(("leaf", "grp")),
        P(("leaf", "grp"), None),
        P(("leaf", "grp"), None),
        P(("leaf", "grp"), None),
        P(),
        P(),
        P(),
    )
    out_specs = P(("leaf", "grp"), None)
    return jax.shard_map(body, mesh=mesh, in_specs=in_specs, out_specs=out_specs, check_vma=False)
```

time: 232 us -> 99.5 us (0.43)
  local copies, waits for them, and re-layouts: 87.3 us -> 20.9 us
  matrix products: 47.8 us -> 0.56 us
  Pallas kernels: 0 us -> 24.5 us
  waiting for transfers between devices: 36.3 us -> 12 us
  other arithmetic: 17.6 us -> 1.43 us
    gather x18 -> x2, local copies, waits for them, and re-layouts: 71.4 us -> 5.13 us  [pick(): rows = jnp.take(table, index.reshape(-1), axis=0, mode='clip')]
    dot_general x20 -> x2, matrix products: 47.8 us -> 0.56 us  [dot(): return jnp.dot(a, b, preferred_element_type=F32)]
    pallas_call x0 -> x4, Pallas kernels: none -> 24.5 us  [the longest x2 12.1 us: own_pass(): pl.pallas_call(functools.partial(own_kernel, first, offsets), out_shape=j...]
    all_to_all x4, waiting for transfers between devices: 36.3 us -> 12 us  [exchange(): return lax.all_to_all(rows, axis, split_axis=0, concat_axis=0, tiled=True)]
    select_n x20 -> x1, other arithmetic: 14.5 us -> 1.25 us  [body(): fine = jnp.where(alive, moments, jnp.zeros((), moments.dtype))]
    dynamic_slice x16 -> x0, local copies, waits for them, and re-layouts: 12.9 us -> none  [body(): far_field, unused = lax.scan(add_offset, start, (pair_source, offset_ops))]
    unnamed x9 -> x38, local copies, waits for them, and re-layouts: 1.92 us -> 14 us
  transfers between devices with their start and end apart: 4 -> 4, of which waited for: 4 -> 3; matrix products, arithmetic and copies ran while one was open for 2% -> 9% of each run, Pallas kernels for 0% -> 22%
where the time goes in v1:
time: 99.5 us; the launch traced here: 98.7 us
  starting transfers between devices  38.5 us (39%)
  Pallas kernels  24.5 us (25%)
  local copies, waits for them, and re-layouts  20.9 us (21%)
  waiting for transfers between devices  12 us (12%)
  other arithmetic  1.43 us (1%)
    all_to_all x4, starting transfers between devices, exchange(): return lax.all_to_all(rows, axis, split_axis=0, concat_axis=0, tiled=True)  38.5 us
    unnamed x38, local copies, waits for them, and re-layouts  14 us
    pallas_call x2, Pallas kernels, own_pass(): pl.pallas_call(functools.partial(own_kernel, first, offsets), out_shape=j...  12.1 us
    all_to_all x4, waiting for transfers between devices, exchange(): return lax.all_to_all(rows, axis, split_axis=0, concat_axis=0, tiled=True)  12 us
    pallas_call x1, Pallas kernels, near_pass(): pl.pallas_call(functools.partial(near_kernel, near_base), out_shape=(jax....  9.3 us
    gather x2, local copies, waits for them, and re-layouts, pick(): rows = jnp.take(table, index.reshape(-1), axis=0, mode='clip')  5.13 us
    pallas_call x1, Pallas kernels, far_pass(): pl.pallas_call(functools.partial(far_kernel, far_base), out_shape=jax.Sha...  3.04 us
  transfers between devices with their start and end apart: 4, of which 3 were waited for; matrix products, arithmetic and copies ran while one was open for 9% of the time, Pallas kernels for 22%

profile of v1, /device:TPU:1, one launch (start us, length us, event | category | flops | bytes accessed | tf_op | source)
XLA Modules:
  0.0 98.7 jit_solution(16428689385005797547)
XLA Ops:
  0.0 1.4 %all_to_all.21 = s32[12,1,32]{2,1,0:T(1,128)} reshape(s32[12,32]{1,0:T(8,128)} %param.10) | data formatting | bytes 3072 | tf_op jit(solution)/shard_map/all_to_all | solution.py:169
  1.4 15.7 %all-to-all-start.2 = ((s32[12,1,32]{2,1,0:T(1,128)}), s32[12,1,32]{2,1,0:T(1,128)S(1)}, u32[]{:S(2)}, u32[]{:S(2)}) async-start(s32[12,1,32]{2,1,0:T(1,128)} %all_to_all.21), calls=%async_computation.2 | async-start | bytes 12288 | tf_op jit(solution)/shard_map/all_to_all | solution.py:169
  17.8 1.2 %broadcast_select_fusion.fine_ref = bf16[1024,256]{1,0:T(8,128)(2,1)S(1)} fusion(bf16[1024,256]{1,0:T(8,128)(2,1)} %param.8, pred[1024]{0:T(1024)(128)(4,1)S(1)} %iota_compare_fusion), kind=kLoop, calls=%fused_computation.5 | loop fusion | flops 262144 | bytes 1049600 | tf_op jit(solution)/shard_map/jit(_where)/select_n | solution.py:188
  19.0 0.2 reshape.47
  19.3 0.3 convolution_convert_fusion.mid_ref
  19.7 0.2 convolution_convert_fusion.1
  20.0 0.5 copy-done.16
  20.5 0.2 copy.13
  20.7 0.8 copy.12
  21.6 4.5 %all-to-all-done.2 = s32[12,1,32]{2,1,0:T(1,128)S(1)} async-done(((s32[12,1,32]{2,1,0:T(1,128)}), s32[12,1,32]{2,1,0:T(1,128)S(1)}, u32[]{:S(2)}, u32[]{:S(2)}) %all-to-all-start.2) | async-done | bytes 1568 | tf_op jit(solution)/shard_map/all_to_all | solution.py:169
  26.1 12.2 %all-to-all-start = ((s32[64,1,8]{2,1,0:T(1,128)}), s32[64,1,8]{2,1,0:T(1,128)S(1)}, u32[]{:S(2)}, u32[]{:S(2)}) async-start(s32[64,1,8]{2,1,0:T(1,128)} %bitcast.2), calls=%async_computation | async-start | bytes 65536 | tf_op jit(solution)/shard_map/all_to_all | solution.py:169
  38.3 2.6 %gather_fusion.1 = bf16[384,256]{1,0:T(8,128)(2,1)} fusion(bf16[1152,256]{1,0:T(8,128)(2,1)S(1)} %pad_maximum_fusion, s32[1024]{0:T(1024)S(1)} %pad_clamp_fusion), kind=kCustom, calls=%fused_computation.1 | custom fusion | bytes 394752 | tf_op jit(solution)/shard_map/jit(_take)/gather | solution.py:173
  40.9 6.6 %all-to-all-done = s32[64,1,8]{2,1,0:T(1,128)S(1)} async-done(((s32[64,1,8]{2,1,0:T(1,128)}), s32[64,1,8]{2,1,0:T(1,128)S(1)}, u32[]{:S(2)}, u32[]{:S(2)}) %all-to-all-start) | async-done | bytes 2080 | tf_op jit(solution)/shard_map/all_to_all | solution.py:169
  47.5 3.8 %all-to-all-start.3 = ((bf16[12,32,256]{2,1,0:T(8,128)(2,1)}), bf16[12,32,256]{2,1,0:T(8,128)(2,1)S(1)}, u32[]{:S(2)}, u32[]{:S(2)}) async-start(bf16[12,32,256]{2,1,0:T(8,128)(2,1)} %bitcast.6), calls=%async_computation.3 | async-start | bytes 393216 | tf_op jit(solution)/shard_map/all_to_all | solution.py:169
  51.3 1.6 %copy-done.1 = bf16[16,256,256]{2,1,0:T(8,128)(2,1)S(1)} copy-done((bf16[16,256,256]{2,1,0:T(8,128)(2,1)S(1)}, bf16[16,256,256]{2,1,0:T(8,128)(2,1)}, u32[]{:S(2)}) %copy-start.1) | copy-done | bytes 2097176
  52.9 6.1 %own_pass.2.refs_0_ = f32[1024,256]{1,0:T(8,128)S(1)} custom-call(bf16[1024,256]{1,0:T(8,128)(2,1)S(1)} %broadcast_select_fusion.fine_ref, s32[1168,16]{1,0:T(8,128)S(1)} %bitcast.16, bf16[16,256,256]{2,1,0:T(8,128)(2,1)S(1)} %copy-done.1), custom_call_target="tpu_custom_call" | custom-call | flops 5368709120 | bytes 4194304 | tf_op jit(solution)/shard_map/own_pass/pallas_call | solution.py:53
  59.0 1.0 copy-done.14
  60.1 2.6 %gather_fusion = bf16[512,256]{1,0:T(8,128)(2,1)} fusion(bf16[144,256]{1,0:T(8,128)(2,1)S(1)} %pad_maximum_fusion.1, s32[1024]{0:T(1024)S(1)} %pad_clamp_fusion.1), kind=kCustom, calls=%fused_computation | custom fusion | bytes 526336 | tf_op jit(solution)/shard_map/jit(_take)/gather | solution.py:173
  62.7 0.8 all-to-all-done.3
  63.6 6.9 %all-to-all-start.1 = ((bf16[64,8,256]{2,1,0:T(8,128)(2,1)}), bf16[64,8,256]{2,1,0:T(8,128)(2,1)S(1)}, u32[]{:S(2)}, u32[]{:S(2)}) async-start(bf16[64,8,256]{2,1,0:T(8,128)(2,1)} %bitcast.3), calls=%async_computation.1 | async-start | bytes 524288 | tf_op jit(solution)/shard_map/all_to_all | solution.py:169
  70.5 1.6 %copy-done.2 = bf16[16,256,256]{2,1,0:T(8,128)(2,1)S(1)} copy-done((bf16[16,256,256]{2,1,0:T(8,128)(2,1)S(1)}, bf16[16,256,256]{2,1,0:T(8,128)(2,1)}, u32[]{:S(2)}) %copy-start.2) | copy-done | bytes 2097176
  72.0 1.2 %copy-done.15 = f32[1024,256]{1,0:T(8,128)S(1)} copy-done((f32[1024,256]{1,0:T(8,128)S(1)}, f32[1024,256]{1,0:T(8,128)}, u32[]{:S(2)}) %copy-start.15) | copy-done | bytes 1048600
  73.3 6.1 %own_pass.3.total_ref = f32[1024,256]{1,0:T(8,128)S(1)} custom-call(bf16[1024,256]{1,0:T(8,128)(2,1)S(1)} %broadcast_select_fusion.fine_ref, s32[1168,16]{1,0:T(8,128)S(1)} %bitcast.17, bf16[16,256,256]{2,1,0:T(8,128)(2,1)S(1)} %copy-done.2, f32[1024,256]{1,0:T(8,128)S(1)} %copy-done.15), custom_call_target="tpu_custom_call" | custom-call | flops 5368709120 | bytes 4194304 | tf_op jit(solution)/shard_map/own_pass/pallas_call | solution.py:53
  79.4 1.1 %copy-done.9 = s32[16,1168]{0,1:T(8,128)S(1)} copy-done((s32[16,1168]{0,1:T(8,128)S(1)}, s32[16,1168]{0,1:T(8,128)}, u32[]{:S(2)}) %copy-start.9) | copy-done | bytes 74776
  80.5 0.9 copy-done.11
  81.4 9.3 %near_pass.1 = (f32[1024,256]{1,0:T(8,128)S(1)}, f32[128,256]{1,0:T(8,128)S(1)}) custom-call(bf16[384,256]{1,0:T(8,128)(2,1)S(1)} %bitcast.20, bf16[128,256]{1,0:T(8,128)(2,1)S(1)} %convolution_convert_fusion.mid_ref, s32[1168,16]{1,0:T(8,128)S(1)} %bitcast.19, bf16[16,256,256]{2,1,0:T(8,128)(2,1)S(1)} %copy-done.3, f32[1024,256]{1,0:T(8,128)S(1)} %own_pass.3.total_ref), custom_call_target="tpu_custom_call" | custom-call | flops 4026531840 | bytes 6291456 | tf_op jit(solution)/shard_map/near_pass/pallas_call | solution.py:95
  90.7 1.0 copy-done.6
  91.7 0.6 copy-done.12
  92.3 1.2 %copy-done.5 = bf16[8,256,256]{2,1,0:T(8,128)(2,1)S(1)} copy-done((bf16[8,256,256]{2,1,0:T(8,128)(2,1)S(1)}, bf16[8,256,256]{2,1,0:T(8,128)(2,1)}, u32[]{:S(2)}) %copy-start.5) | copy-done | bytes 1048600
  93.6 1.2 %copy-done.7 = f32[1024,256]{1,0:T(8,128)S(1)} copy-done((f32[1024,256]{1,0:T(8,128)S(1)}, f32[1024,256]{1,0:T(8,128)}, u32[]{:S(2)}) %copy-start.7) | copy-done | bytes 1048600
  94.8 0.9 copy-done.13
  95.7 3.0 %far_pass.1 = bf16[1024,256]{1,0:T(8,128)(2,1)} custom-call(s32[1]{0:T(128)} %copy.14.live_ref, bf16[512,256]{1,0:T(8,128)(2,1)S(1)} %bitcast.15, s32[144,16]{1,0:T(8,128)S(1)} %slice.8.pairs_ref, bf16[16,256,256]{2,1,0:T(8,128)(2,1)S(1)} %copy-done.4, bf16[8,256,256]{2,1,0:T(8,128)(2,1)S(1)} %copy-done.5, f32[128,256]{1,0:T(8,128)S(1)} %copy-done.13, ...), custom_call_target="tpu_custom_call" | custom-call | flops 1040187392 | bytes 6291456 | tf_op jit(solution)/shard_map/far_pass/pallas_call | solution.py:152
  (36 shorter events, 0.5 us)
Async XLA Ops:
  0.0 19.3 %copy-start = (bf16[8,256,256]{2,1,0:T(8,128)(2,1)S(1)}, bf16[8,256,256]{2,1,0:T(8,128)(2,1)}, u32[]{:S(2)}) copy-start(bf16[8,256,256]{2,1,0:T(8,128)(2,1)} %param.13) | copy-start | bytes 3145732
  1.4 24.7 %all-to-all-start.2 = ((s32[12,1,32]{2,1,0:T(1,128)}), s32[12,1,32]{2,1,0:T(1,128)S(1)}, u32[]{:S(2)}, u32[]{:S(2)}) async-start(s32[12,1,32]{2,1,0:T(1,128)} %all_to_all.21), calls=%async_computation.2 | async-start | bytes 12288 | tf_op jit(solution)/shard_map/all_to_all | solution.py:169
  19.6 0.9 copy-start.16
  19.6 1.1 %copy-start.17 = (s32[64,8]{0,1:T(8,128)S(1)}, s32[64,8]{0,1:T(8,128)}, u32[]{:S(2)}) copy-start(s32[64,8]{0,1:T(8,128)} %param.11) | copy-start | bytes 6148
  20.7 58.6 %copy-start.8 = (s32[16,1168]{0,1:T(8,128)}, s32[16,1168]{0,1:T(8,128)S(1)}, u32[]{:S(2)}) copy-start(s32[16,1168]{0,1:T(8,128)S(1)} %copy.13) | copy-start | bytes 224260
  26.1 21.5 %all-to-all-start = ((s32[64,1,8]{2,1,0:T(1,128)}), s32[64,1,8]{2,1,0:T(1,128)S(1)}, u32[]{:S(2)}, u32[]{:S(2)}) async-start(s32[64,1,8]{2,1,0:T(1,128)} %bitcast.2), calls=%async_computation | async-start | bytes 65536 | tf_op jit(solution)/shard_map/all_to_all | solution.py:169
  47.5 16.0 %all-to-all-start.3 = ((bf16[12,32,256]{2,1,0:T(8,128)(2,1)}), bf16[12,32,256]{2,1,0:T(8,128)(2,1)S(1)}, u32[]{:S(2)}, u32[]{:S(2)}) async-start(bf16[12,32,256]{2,1,0:T(8,128)(2,1)} %bitcast.6), calls=%async_computation.3 | async-start | bytes 393216 | tf_op jit(solution)/shard_map/all_to_all | solution.py:169
  51.3 1.6 %copy-start.1 = (bf16[16,256,256]{2,1,0:T(8,128)(2,1)S(1)}, bf16[16,256,256]{2,1,0:T(8,128)(2,1)}, u32[]{:S(2)}) copy-start(bf16[16,256,256]{2,1,0:T(8,128)(2,1)} %ops_ref.7) | copy-start | bytes 6291460
  59.0 1.0 %copy-start.14 = (f32[1024,256]{1,0:T(8,128)}, f32[1024,256]{1,0:T(8,128)S(1)}, u32[]{:S(2)}) copy-start(f32[1024,256]{1,0:T(8,128)S(1)} %own_pass.2.refs_0_) | copy-start | bytes 3145732
  63.5 15.8 %copy-start.10 = (bf16[12,32,256]{2,1,0:T(8,128)(2,1)}, bf16[12,32,256]{2,1,0:T(8,128)(2,1)S(1)}, u32[]{:S(2)}) copy-start(bf16[12,32,256]{2,1,0:T(8,128)(2,1)S(1)} %all-to-all-done.3) | copy-start | bytes 589828
  63.6 28.8 %all-to-all-start.1 = ((bf16[64,8,256]{2,1,0:T(8,128)(2,1)}), bf16[64,8,256]{2,1,0:T(8,128)(2,1)S(1)}, u32[]{:S(2)}, u32[]{:S(2)}) async-start(bf16[64,8,256]{2,1,0:T(8,128)(2,1)} %bitcast.3), calls=%async_computation.1 | async-start | bytes 524288 | tf_op jit(solution)/shard_map/all_to_all | solution.py:169
  70.4 1.6 %copy-start.2 = (bf16[16,256,256]{2,1,0:T(8,128)(2,1)S(1)}, bf16[16,256,256]{2,1,0:T(8,128)(2,1)}, u32[]{:S(2)}) copy-start(bf16[16,256,256]{2,1,0:T(8,128)(2,1)} %ops_ref.7) | copy-start | bytes 6291460
  72.0 1.2 %copy-start.15 = (f32[1024,256]{1,0:T(8,128)S(1)}, f32[1024,256]{1,0:T(8,128)}, u32[]{:S(2)}) copy-start(f32[1024,256]{1,0:T(8,128)} %copy-done.14) | copy-start | bytes 3145732
  73.3 6.1 %copy-start.3 = (bf16[16,256,256]{2,1,0:T(8,128)(2,1)S(1)}, bf16[16,256,256]{2,1,0:T(8,128)(2,1)}, u32[]{:S(2)}) copy-start(bf16[16,256,256]{2,1,0:T(8,128)(2,1)} %ops_ref.7) | copy-start | bytes 6291460
  79.4 1.1 %copy-start.9 = (s32[16,1168]{0,1:T(8,128)S(1)}, s32[16,1168]{0,1:T(8,128)}, u32[]{:S(2)}) copy-start(s32[16,1168]{0,1:T(8,128)} %copy-done.8) | copy-start | bytes 224260
  80.5 0.9 copy-start.11
  81.4 11.0 %copy-start.4 = (bf16[16,256,256]{2,1,0:T(8,128)(2,1)S(1)}, bf16[16,256,256]{2,1,0:T(8,128)(2,1)}, u32[]{:S(2)}) copy-start(bf16[16,256,256]{2,1,0:T(8,128)(2,1)} %ops_ref.7) | copy-start | bytes 6291460
  90.7 1.0 %copy-start.6 = (f32[1024,256]{1,0:T(8,128)}, f32[1024,256]{1,0:T(8,128)S(1)}, u32[]{:S(2)}) copy-start(f32[1024,256]{1,0:T(8,128)S(1)} %get-tuple-element.8.total_ref) | copy-start | bytes 3145732
  91.7 0.7 copy-start.12
  92.3 1.2 %copy-start.5 = (bf16[8,256,256]{2,1,0:T(8,128)(2,1)S(1)}, bf16[8,256,256]{2,1,0:T(8,128)(2,1)}, u32[]{:S(2)}) copy-start(bf16[8,256,256]{2,1,0:T(8,128)(2,1)} %down_ref.1) | copy-start | bytes 3145732
  93.6 1.2 %copy-start.7 = (f32[1024,256]{1,0:T(8,128)S(1)}, f32[1024,256]{1,0:T(8,128)}, u32[]{:S(2)}) copy-start(f32[1024,256]{1,0:T(8,128)} %copy-done.6) | copy-start | bytes 3145732
  94.8 0.9 copy-start.13

commit v2 on v0

v2 whole, which is shorter than its diff:
```python
import functools

import jax
import jax.numpy as jnp
from jax import lax
from jax.experimental import pallas as pl
from jax.experimental.pallas import tpu as pltpu
from jax.sharding import PartitionSpec as P

BF16 = jnp.bfloat16
F32 = jnp.float32
I32 = jnp.int32
TILE = 256
EARLY = 4
ANY = pl.BlockSpec(memory_space=pl.ANY)
VMEM = pl.BlockSpec(memory_space=pltpu.VMEM)
SMEM = pl.BlockSpec(memory_space=pltpu.SMEM)
TIGHT = pltpu.CompilerParams(vmem_limit_bytes=53000 << 10)
PARAMS = pltpu.CompilerParams(vmem_limit_bytes=56 << 20)


def one_hot(columns, first, width):
    rows = columns[0].shape[0]
    wide = [jnp.broadcast_to(column, (rows, 128)).astype(jnp.int16) for column in columns]
    lane = lax.broadcasted_iota(I32, (rows, 128), 1).astype(jnp.int16)
    one = jnp.ones((rows, 128), BF16)
    zero = jnp.zeros((rows, 128), BF16)
    parts = []
    for k in range(width // 128):
        here = lane + jnp.int16(first + 128 * k)
        hit = wide[0] == here
        for other in wide[1:]:
            hit = hit | (other == here)
        parts.append(jnp.where(hit, one, zero))
    return parts[0] if len(parts) == 1 else jnp.concatenate(parts, axis=1)


def dot(a, b):
    return jnp.dot(a, b, preferred_element_type=F32)


def cost(macs, size):
    return pl.CostEstimate(flops=2 * macs, bytes_accessed=size, transcendentals=0)


def start(src, dst, sem):
    copy = pltpu.make_async_copy(src, dst, sem)
    copy.start()
    return copy


def up_kernel(live_ref, source_ref, moments_in, up_in, fine_out, high_out, pairs_out,
              fine, up, high, pairs, wide, sems):
    count, size = fine.shape
    middles = count // 8
    get_fine = start(moments_in, fine, sems.at[0])
    get_up = start(up_in, up, sems.at[1])
    cells = pairs.shape[0]
    for low in range(0, cells, 128):
        block = source_ref[:, low : min(low + 128, cells)]
        there = block.shape[1]
        if there < 128:
            block = jnp.concatenate([block, jnp.zeros((block.shape[0], 128 - there), I32)], axis=1)
        pairs[low : low + there, :] = block.T[:there, :]
    put_pairs = start(pairs, pairs_out, sems.at[2])
    live = live_ref[0]
    get_fine.wait()
    for m in range(count // TILE):
        rows = slice(m * TILE, (m + 1) * TILE)
        row = lax.broadcasted_iota(I32, (TILE, 1), 0) + m * TILE
        kept = jnp.where(row < live, fine[rows, :].astype(F32), 0.0)
        fine[rows, :] = kept.astype(BF16)
        for h in range(2):
            wide[h, rows, :] = kept[:, 128 * h : 128 * h + 128]
    put_fine = start(fine, fine_out, sems.at[0])
    get_up.wait()

    def merge(parents):
        total = None
        for k in range(8):
            rows = pl.ds(k, parents, stride=8)
            child = jnp.concatenate([wide[0, rows, :], wide[1, rows, :]], axis=1).astype(BF16)
            term = dot(child, up[k])
            total = term if total is None else total + term
        return total.astype(BF16)

    middle = merge(middles)
    high[:middles, :] = middle
    for h in range(2):
        wide[h, :middles, :] = middle[:, 128 * h : 128 * h + 128].astype(F32)
    high[middles:, :] = merge(middles // 8)
    put_high = start(high, high_out, sems.at[1])
    for put in (put_pairs, put_fine, put_high):
        put.wait()


def up_pass(live, source, moments, up):
    count, size = moments.shape
    offsets, cells = source.shape
    upper = cells - count
    return pl.pallas_call(
        up_kernel,
        out_shape=(
            jax.ShapeDtypeStruct((count, size), BF16),
            jax.ShapeDtypeStruct((upper, size), BF16),
            jax.ShapeDtypeStruct((cells, offsets), I32),
        ),
        in_specs=[SMEM, VMEM, ANY, ANY],
        out_specs=(ANY, ANY, ANY),
        scratch_shapes=[
            pltpu.VMEM((count, size), BF16),
            pltpu.VMEM(up.shape, BF16),
            pltpu.VMEM((upper, size), BF16),
            pltpu.VMEM((cells, offsets), I32),
            pltpu.VMEM((2, count, 128), F32),
            pltpu.SemaphoreType.DMA((3,)),
        ],
        compiler_params=PARAMS,
        cost_estimate=cost(count * size * size, 3 << 20),
        name="up_pass",
    )(live, source, moments, up)


def own_kernel(first, low, offsets, asked_ref, *refs):
    if first:
        fine_in, high_in, pairs_in, ops_in, picked_out, total_out = refs[:6]
        refs = refs[6:]
    else:
        fine_in, high_in, pairs_in, ops_in, total_in, picked_out, total_out = refs[:7]
        refs = refs[7:]
    table, pairs, ops, total, moved, wide, picked, sems = refs
    count = total.shape[0]
    upper = high_in.shape[0]
    steps = len(offsets)
    gets = [
        start(fine_in, table.at[pl.ds(0, count)], sems.at[0]),
        start(high_in, table.at[pl.ds(count, upper)], sems.at[1]),
        start(pairs_in, pairs, sems.at[2]),
        start(ops_in.at[pl.ds(offsets[0], steps)], ops, sems.at[3]),
    ]
    if not first:
        gets.append(start(total_in, total, sems.at[4]))
    end = table.shape[0]
    table[count + upper : end, :] = jnp.zeros((end - count - upper, table.shape[1]), BF16)
    peers, unit, slots = asked_ref.shape
    wide[...] = jnp.zeros(wide.shape, I32)
    for p in range(peers):
        wide[p : p + 1, :slots] = asked_ref[p]
    asked = wide[...].T - low
    for get in gets:
        get.wait()
    span = end - low
    if slots % 16 == 0:
        hot = jnp.concatenate(
            [one_hot([asked[:slots, p : p + 1]], 0, span) for p in range(peers)], axis=0
        )
    else:
        lane = lax.broadcasted_iota(I32, (slots, span), 1)
        hot = jnp.concatenate(
            [jnp.where(asked[:slots, p : p + 1] == lane, 1.0, 0.0) for p in range(peers)], axis=0
        ).astype(BF16)
    picked[...] = dot(hot, table[low:end, :]).astype(BF16)
    puts = [start(picked, picked_out, sems.at[0])]
    for n, o in enumerate(offsets):
        moved[n % 2] = dot(table[:count, :], ops[n]).astype(BF16)
        for m in range(count // TILE):
            rows = slice(m * TILE, (m + 1) * TILE)
            part = dot(one_hot([pairs[rows, o : o + 1]], 0, count), moved[n % 2])
            if n > 0 or not first:
                part = part + total[rows, :]
            total[rows, :] = part
    puts.append(start(total, total_out, sems.at[1]))
    for put in puts:
        put.wait()


def own_pass(low, asked, fine, high, pairs, ops, offsets, total):
    count, size = fine.shape
    first = total is None
    args = (asked, fine, high, pairs, ops) + (() if first else (total,))
    steps = len(offsets)
    replies = asked.shape[0] * asked.shape[2]
    return pl.pallas_call(
        functools.partial(own_kernel, first, low, offsets),
        out_shape=(
            jax.ShapeDtypeStruct((replies, size), BF16),
            jax.ShapeDtypeStruct((count, size), F32),
        ),
        in_specs=[VMEM] + [ANY] * (len(args) - 1),
        out_specs=(ANY, ANY),
        scratch_shapes=[
            pltpu.VMEM((count + 256, size), BF16),
            pltpu.VMEM(pairs.shape, I32),
            pltpu.VMEM((steps, size, size), BF16),
            pltpu.VMEM((count, size), F32),
            pltpu.VMEM((2, count, size), BF16),
            pltpu.VMEM((128, 128), I32),
            pltpu.VMEM((replies, size), BF16),
            pltpu.SemaphoreType.DMA((5,)),
        ],
        compiler_params=PARAMS,
        cost_estimate=cost(steps * count * size * (size + count), 4 << 20),
        name="own_pass",
    )(*args)


def near_kernel(base, asked, near_in, high_in, pairs_in, ops_in, total_in, sums_out,
                near, table, pairs, ops, total, moved, picked, sems):
    fine_slots, slots = asked
    groups = near.shape[0] // slots
    mid_slots = slots - fine_slots
    count = total_in.shape[0]
    middles = count // 8
    offsets = ops.shape[0]
    near_fine = groups * fine_slots
    near_mid = groups * mid_slots
    gets = [
        start(near_in, near, sems.at[0]),
        start(ops_in, ops, sems.at[1]),
        start(pairs_in, pairs, sems.at[2]),
        start(high_in.at[pl.ds(0, middles)], table.at[pl.ds(0, middles)], sems.at[3]),
        start(total_in, total.at[pl.ds(0, count)], sems.at[4]),
    ]
    for get in gets:
        get.wait()
    fines = jnp.concatenate(
        [near[g * slots : g * slots + fine_slots, :] for g in range(groups)], axis=0
    )
    for o in range(offsets):
        moved[o * near_fine : (o + 1) * near_fine, :] = dot(fines, ops[o]).astype(BF16)
    offset = lax.broadcasted_iota(I32, (TILE, offsets), 1) * near_fine
    width = 1536
    for m in range(count // TILE):
        rows = slice(m * TILE, (m + 1) * TILE)
        slot = pairs[rows, :] - base
        place = (slot >> 5) * fine_slots + (slot & (slots - 1)) + offset
        place = jnp.where((slot >= 0) & (slot < groups * slots), place, -1)
        part = total[rows, :]
        for first in range(0, offsets * near_fine, width):
            pieces = []
            for low in range(first, first + width, 128):
                touched = range(low // near_fine, (low + 127) // near_fine + 1)
                pieces.append(one_hot([place[:, o : o + 1] for o in touched], low, 128))
            part = part + dot(jnp.concatenate(pieces, axis=1), moved[first : first + width, :])
        total[rows, :] = part
    fines_in = pl.ds(0, count)
    puts = [start(total.at[fines_in], sums_out.at[fines_in], sems.at[0])]
    table[middles : middles + near_mid, :] = jnp.concatenate(
        [near[g * slots + fine_slots : (g + 1) * slots, :] for g in range(groups)], axis=0
    )
    table[middles + near_mid :, :] = jnp.zeros((table.shape[0] - middles - near_mid, table.shape[1]), BF16)
    source = pairs[count : count + middles, :]
    slot = source - base
    place = middles + (slot >> 5) * mid_slots + (slot & (slots - 1)) - fine_slots
    place = jnp.where((slot >= 0) & (slot < groups * slots), place, -1)
    place = jnp.where(slot < 0, source - count, place)
    for o in range(offsets):
        hot = one_hot([place[:, o : o + 1]], 0, table.shape[0])
        picked[o] = dot(hot, table[...]).astype(BF16)
    field = dot(picked[0], ops[0])
    for o in range(1, offsets):
        field = field + dot(picked[o], ops[o])
    total[count:, :] = field
    mids_in = pl.ds(count, middles)
    puts.append(start(total.at[mids_in], sums_out.at[mids_in], sems.at[1]))
    for put in puts:
        put.wait()


def near_pass(base, asked, near, high, pairs, ops, total):
    count, size = total.shape
    middles = count // 8
    offsets = ops.shape[0]
    near_fine = near.shape[0] // asked[1] * asked[0]
    macs = offsets * near_fine * size * (size + count) + 3 * offsets * middles * size * size
    return pl.pallas_call(
        functools.partial(near_kernel, base, asked),
        out_shape=jax.ShapeDtypeStruct((count + middles, size), F32),
        in_specs=[ANY] * 5,
        out_specs=ANY,
        scratch_shapes=[
            pltpu.VMEM(near.shape, BF16),
            pltpu.VMEM((256, size), BF16),
            pltpu.VMEM(pairs.shape, I32),
            pltpu.VMEM(ops.shape, BF16),
            pltpu.VMEM((count + middles, size), F32),
            pltpu.VMEM((offsets * near_fine, size), BF16),
            pltpu.VMEM((offsets, middles, size), BF16),
            pltpu.SemaphoreType.DMA((5,)),
        ],
        compiler_params=PARAMS,
        cost_estimate=cost(macs, 6 << 20),
        name="near_pass",
    )(near, high, pairs, ops, total)


def far_kernel(base, live_ref, far_ref, pairs_in, ops_in, down_in, sums_in, out_out,
               pairs, ops, down, mid, total, out, picked, mid_wide, fine_wide, sems, out_sems):
    count = total.shape[0]
    middles = mid.shape[0]
    cells = pairs.shape[0]
    offsets = ops.shape[0]
    get_pairs = start(pairs_in.at[pl.ds(count, cells)], pairs, sems.at[0])
    get_ops = start(ops_in, ops, sems.at[1])
    get_mid = start(sums_in.at[pl.ds(count, middles)], mid, sems.at[2])
    get_down = start(down_in, down, sems.at[3])
    get_total = start(sums_in.at[pl.ds(0, count)], total, sems.at[4])
    get_pairs.wait()
    place = pairs[...] - base
    for o in range(offsets):
        hot = one_hot([place[:, o : o + 1]], 0, far_ref.shape[0])
        picked[o] = dot(hot, far_ref[...]).astype(BF16)
    get_ops.wait()
    field = dot(picked[0], ops[0])
    for o in range(1, offsets):
        field = field + dot(picked[o], ops[o])
    get_mid.wait()
    get_down.wait()
    coarse = field[middles:, :].astype(BF16)
    for k in range(8):
        rows = pl.ds(k, cells - middles, stride=8)
        spread = dot(coarse, down[k])
        mid_wide[0, rows, :] = spread[:, :128]
        mid_wide[1, rows, :] = spread[:, 128:]
    spread = jnp.concatenate([mid_wide[0], mid_wide[1]], axis=1)
    local = (field[:middles, :] + mid[...] + spread).astype(BF16)
    for k in range(8):
        rows = pl.ds(k, middles, stride=8)
        spread = dot(local, down[k])
        fine_wide[0, rows, :] = spread[:, :128]
        fine_wide[1, rows, :] = spread[:, 128:]
    get_total.wait()
    live = live_ref[0]
    puts = []
    for m in range(count // TILE):
        rows = slice(m * TILE, (m + 1) * TILE)
        row = lax.broadcasted_iota(I32, (TILE, 1), 0) + m * TILE
        spread = jnp.concatenate([fine_wide[0, rows, :], fine_wide[1, rows, :]], axis=1)
        out[rows, :] = jnp.where(row < live, total[rows, :] + spread, 0.0).astype(BF16)
        puts.append(start(out.at[pl.ds(m * TILE, TILE)], out_out.at[pl.ds(m * TILE, TILE)], out_sems.at[m]))
    for put in puts:
        put.wait()


def far_pass(base, live, far, pairs, ops, down, sums):
    size = sums.shape[1]
    count = sums.shape[0] // 9 * 8
    middles = count // 8
    cells = pairs.shape[0] - count
    offsets = ops.shape[0]
    macs = offsets * cells * size * (far.shape[0] + size) + count * size * size
    return pl.pallas_call(
        functools.partial(far_kernel, base),
        out_shape=jax.ShapeDtypeStruct((count, size), BF16),
        in_specs=[SMEM, VMEM] + [ANY] * 4,
        out_specs=ANY,
        scratch_shapes=[
            pltpu.VMEM((cells, pairs.shape[1]), I32),
            pltpu.VMEM(ops.shape, BF16),
            pltpu.VMEM(down.shape, BF16),
            pltpu.VMEM((middles, size), F32),
            pltpu.VMEM((count, size), F32),
            pltpu.VMEM((count, size), BF16),
            pltpu.VMEM((offsets, cells, size), BF16),
            pltpu.VMEM((2, middles, 128), F32),
            pltpu.VMEM((2, count, 128), F32),
            pltpu.SemaphoreType.DMA((5,)),
            pltpu.SemaphoreType.DMA((count // TILE,)),
        ],
        compiler_params=TIGHT,
        cost_estimate=cost(macs, 6 << 20),
        name="far_pass",
    )(live, far, pairs, ops, down, sums)


def exchange(rows, axis):
    return lax.all_to_all(rows, axis, split_axis=0, concat_axis=0, tiled=True)


def after(value, *others):
    return lax.optimization_barrier((value,) + others)[0]


def body(
    moments, live_fine, near_requests, far_requests, pair_source, child_up, child_down, offset_ops
):
    fine_count, size = moments.shape
    offsets, cells = pair_source.shape
    slots = near_requests.shape[1]
    early = tuple(range(EARLY))
    late = tuple(range(EARLY, offsets))
    near_asked = exchange(near_requests[:, None, :], "grp")
    fine, high, pairs = up_pass(live_fine, pair_source, moments, child_up)
    far_asked = exchange(after(far_requests, high)[:, None, :], "leaf")
    replies, total = own_pass(0, near_asked, fine, high, pairs, offset_ops, early, None)
    near_tiles = exchange(replies.reshape(-1, slots, size), "grp").reshape(-1, size)
    replies, total = own_pass(
        fine_count, far_asked, fine, high, pairs, offset_ops, late, total
    )
    far_tiles = exchange(replies.reshape(far_requests.shape + (size,)), "leaf").reshape(-1, size)
    sums = near_pass(
        cells, (slots * 3 // 4, slots), near_tiles, high, pairs, offset_ops, total
    )
    far_base = cells + near_tiles.shape[0]
    return far_pass(far_base, live_fine, far_tiles, pairs, offset_ops, child_down, sums)


def solution(mesh):
    axes = ("leaf", "grp")
    in_specs = (
        P(axes, None),
        P(axes),
        P(axes, None),
        P(axes, None),
        P(axes, None),
        P(),
        P(),
        P(),
    )
    return jax.shard_map(
        body, mesh=mesh, in_specs=in_specs, out_specs=P(axes, None), check_vma=False
    )
```

time: 232 us -> 92.9 us (0.40); the launches traced: 229 us -> 92.2 us
  local copies, waits for them, and re-layouts: 87.3 us -> 2.68 us
  matrix products: 47.8 us -> 0 us
  Pallas kernels: 0 us -> 34.6 us
  waiting for transfers between devices: 36.3 us -> 11.8 us
  other arithmetic: 17.6 us -> 0 us
  starting transfers between devices: 38.7 us -> 42.2 us
    gather x18 -> x0, local copies, waits for them, and re-layouts: 71.4 us -> none  [the longest x16 67.4 us: add_offset(): picked = jnp.take(sources, rows, axis=0)]
    dot_general x20 -> x0, matrix products: 47.8 us -> none  [the longest x16 44.1 us: add_offset(): jnp.dot(picked, operator, preferred_element_type=jnp.float32)]
    pallas_call x0 -> x5, Pallas kernels: none -> 34.6 us  [the longest x2 19.4 us: own_pass(): pl.pallas_call(functools.partial(own_kernel, first, low, offsets), out_sh...]
    all_to_all x4, waiting for transfers between devices: 36.3 us -> 11.8 us  [exchange(): return lax.all_to_all(rows, axis, split_axis=0, concat_axis=0, tiled=True)]
    select_n x20 -> x0, other arithmetic: 14.5 us -> none  [the longest x16 12.9 us: add_offset(): picked = jnp.take(sources, rows, axis=0)]
    dynamic_slice x16 -> x0, local copies, waits for them, and re-layouts: 12.9 us -> none  [body(): far_field, unused = lax.scan(add_offset, start, (pair_source, offset_ops))]
    all_to_all x4, starting transfers between devices: 38.7 us -> 42.2 us  [exchange(): return lax.all_to_all(rows, axis, split_axis=0, concat_axis=0, tiled=True)]
  transfers between devices with their start and end apart: 4 -> 4, of which waited for: 4 -> 3; matrix products, arithmetic and copies ran while one was open for 2% -> 1% of each run, Pallas kernels for 0% -> 33%
where the time goes in v2:
time: 92.9 us; the launch traced here: 92.2 us
  starting transfers between devices  42.2 us (45%)
  Pallas kernels  34.6 us (37%)
  waiting for transfers between devices  11.8 us (13%)
  local copies, waits for them, and re-layouts  2.68 us (3%)
  between operations  0.95 us (1%)
    all_to_all x4, starting transfers between devices, exchange(): return lax.all_to_all(rows, axis, split_axis=0, concat_axis=0, tiled=True)  42.2 us
    pallas_call x2, Pallas kernels, own_pass(): pl.pallas_call(functools.partial(own_kernel, first, low, offsets), out_sh...  19.4 us
    all_to_all x4, waiting for transfers between devices, exchange(): return lax.all_to_all(rows, axis, split_axis=0, concat_axis=0, tiled=True)  11.8 us
    pallas_call x1, Pallas kernels, near_pass(): pl.pallas_call(functools.partial(near_kernel, base, asked), out_shape=jax...  7.14 us
    pallas_call x1, Pallas kernels, far_pass(): pl.pallas_call(functools.partial(far_kernel, base), out_shape=jax.ShapeDt...  4.08 us
    pallas_call x1, Pallas kernels, up_pass(): pl.pallas_call(up_kernel, out_shape=(jax.ShapeDtypeStruct((count, size),...  3.93 us
  transfers between devices with their start and end apart: 4, of which 3 were waited for; matrix products, arithmetic and copies ran while one was open for 1% of the time, Pallas kernels for 33%

profile of v2, /device:TPU:1, one launch (start us, length us, event | category | flops | bytes accessed | tf_op | source)
XLA Modules:
  0.0 92.2 jit_solution(14901048601634515002)
XLA Ops:
  0.0 1.3 %broadcast_in_dim.7 = s32[12,1,32]{2,1,0:T(1,128)} reshape(s32[12,32]{1,0:T(8,128)} %param.10) | data formatting | bytes 3072 | tf_op jit(solution)/shard_map/broadcast_in_dim | solution.py:392
  1.3 15.7 %all-to-all-start.1 = ((s32[12,1,32]{2,1,0:T(1,128)}), s32[12,1,32]{2,1,0:T(1,128)S(1)}, u32[]{:S(2)}, u32[]{:S(2)}) async-start(s32[12,1,32]{2,1,0:T(1,128)} %broadcast_in_dim.7), calls=%async_computation.1 | async-start | bytes 12288 | tf_op jit(solution)/shard_map/all_to_all | solution.py:377
  17.7 3.9 %up_pass.1 = (bf16[1024,256]{1,0:T(8,128)(2,1)}, bf16[144,256]{1,0:T(8,128)(2,1)}, s32[1168,16]{1,0:T(8,128)}) custom-call(s32[1]{0:T(128)S(6)} %copy.10.live_ref, s32[16,1168]{1,0:T(8,128)} %source_ref.1, bf16[1024,256]{1,0:T(8,128)(2,1)} %moments_in.1, bf16[8,256,256]{2,1,0:T(8,128)(2,1)} %up_in.1), custom_call_target="tpu_custom_call" | custom-call | flops 134217728 | bytes 3145728 | tf_op jit(solution)/shard_map/up_pass/pallas_call | solution.py:101
  21.6 1.4 %copy.9 = s32[64,8]{1,0:T(8,128)} copy(s32[64,8]{0,1:T(8,128)} %param.11) | data formatting | bytes 4096 | tf_op jit(solution)/shard_map/optimization_barrier | solution.py:381
  23.0 3.0 %all-to-all-done.1.asked_ref = s32[12,1,32]{2,1,0:T(1,128)S(1)} async-done(((s32[12,1,32]{2,1,0:T(1,128)}), s32[12,1,32]{2,1,0:T(1,128)S(1)}, u32[]{:S(2)}, u32[]{:S(2)}) %all-to-all-start.1) | async-done | bytes 1568 | tf_op jit(solution)/shard_map/all_to_all | solution.py:377
  25.9 0.0 copy-start.4
  25.9 12.3 %all-to-all-start = ((s32[64,1,8]{2,1,0:T(1,128)}), s32[64,1,8]{2,1,0:T(1,128)S(1)}, u32[]{:S(2)}, u32[]{:S(2)}) async-start(s32[64,1,8]{2,1,0:T(1,128)} %bitcast), calls=%async_computation | async-start | bytes 65536 | tf_op jit(solution)/shard_map/all_to_all | solution.py:377
  38.2 0.0 copy-done.4
  38.2 6.5 %own_pass.2 = (bf16[384,256]{1,0:T(8,128)(2,1)}, f32[1024,256]{1,0:T(8,128)}) custom-call(s32[12,1,32]{2,1,0:T(1,128)} %copy-done.4, bf16[1024,256]{1,0:T(8,128)(2,1)} %get-tuple-element.15.refs_0_, bf16[144,256]{1,0:T(8,128)(2,1)} %get-tuple-element.13.refs_1_.high_in, s32[1168,16]{1,0:T(8,128)} %get-tuple-element.16.refs_2_.pairs_in, ...), custom_call_target="tpu_custom_call" | custom-call | flops 2684354560 | bytes 4194304 | tf_op jit(solution)/shard_map/own_pass/pallas_call | solution.py:183
  44.7 2.9 %all-to-all-done.asked_ref = s32[64,1,8]{2,1,0:T(1,128)S(1)} async-done(((s32[64,1,8]{2,1,0:T(1,128)}), s32[64,1,8]{2,1,0:T(1,128)S(1)}, u32[]{:S(2)}, u32[]{:S(2)}) %all-to-all-start) | async-done | bytes 2080 | tf_op jit(solution)/shard_map/all_to_all | solution.py:377
  47.6 0.0 copy-start.3
  47.6 5.2 %all-to-all-start.3 = ((bf16[12,32,256]{2,1,0:T(8,128)(2,1)}), bf16[12,32,256]{2,1,0:T(8,128)(2,1)S(1)}, u32[]{:S(2)}, u32[]{:S(2)}) async-start(bf16[12,32,256]{2,1,0:T(8,128)(2,1)} %bitcast.8), calls=%async_computation.3 | async-start | bytes 393216 | tf_op jit(solution)/shard_map/all_to_all | solution.py:377
  52.8 0.0 copy-done.3
  52.8 12.9 %own_pass.3 = (bf16[512,256]{1,0:T(8,128)(2,1)}, f32[1024,256]{1,0:T(8,128)}) custom-call(s32[64,1,8]{2,1,0:T(1,128)} %copy-done.3, bf16[1024,256]{1,0:T(8,128)(2,1)} %get-tuple-element.15.refs_0_, bf16[144,256]{1,0:T(8,128)(2,1)} %get-tuple-element.13.refs_1_.high_in, s32[1168,16]{1,0:T(8,128)} %get-tuple-element.16.refs_2_.pairs_in, ...), custom_call_target="tpu_custom_call" | custom-call | flops 8053063680 | bytes 4194304 | tf_op jit(solution)/shard_map/own_pass/pallas_call | solution.py:183
  65.7 0.0 all-to-all-done.3
  65.7 0.0 copy-start.2
  65.7 9.0 %all-to-all-start.2 = ((bf16[64,8,256]{2,1,0:T(8,128)(2,1)}), bf16[64,8,256]{2,1,0:T(8,128)(2,1)S(1)}, u32[]{:S(2)}, u32[]{:S(2)}) async-start(bf16[64,8,256]{2,1,0:T(8,128)(2,1)} %bitcast.6), calls=%async_computation.2 | async-start | bytes 524288 | tf_op jit(solution)/shard_map/all_to_all | solution.py:377
  74.8 0.0 copy-done.2
  74.8 0.0 copy-start
  74.8 0.0 copy-start.1
  74.8 7.1 %near_pass.1.sums_in = f32[1152,256]{1,0:T(8,128)} custom-call(bf16[384,256]{1,0:T(8,128)(2,1)} %bitcast.7, bf16[144,256]{1,0:T(8,128)(2,1)} %get-tuple-element.13.refs_1_.high_in, s32[1168,16]{1,0:T(8,128)} %get-tuple-element.16.refs_2_.pairs_in, bf16[16,256,256]{2,1,0:T(8,128)(2,1)} %ops_in.3, f32[1024,256]{1,0:T(8,128)} %get-tuple-element.20.total_in), custom_call_target="tpu_custom_call" | custom-call | flops 3825205248 | bytes 6291456 | tf_op jit(solution)/shard_map/near_pass/pallas_call | solution.py:276
  82.0 6.0 %all-to-all-done.2 = bf16[64,8,256]{2,1,0:T(8,128)(2,1)S(1)} async-done(((bf16[64,8,256]{2,1,0:T(8,128)(2,1)}), bf16[64,8,256]{2,1,0:T(8,128)(2,1)S(1)}, u32[]{:S(2)}, u32[]{:S(2)}) %all-to-all-start.2) | async-done | bytes 262176 | tf_op jit(solution)/shard_map/all_to_all | solution.py:377
  88.0 0.0 copy-done
  88.0 0.0 copy-done.1
  88.0 4.1 %far_pass.1 = bf16[1024,256]{1,0:T(8,128)(2,1)} custom-call(s32[1]{0:T(128)S(6)} %copy.10.live_ref, bf16[512,256]{1,0:T(8,128)(2,1)S(1)} %bitcast.5, s32[1168,16]{1,0:T(8,128)S(1)} %copy-done.1, bf16[16,256,256]{2,1,0:T(8,128)(2,1)} %ops_in.3, bf16[8,256,256]{2,1,0:T(8,128)(2,1)S(1)} %copy-done, f32[1152,256]{1,0:T(8,128)} %near_pass.1.sums_in), custom_call_target="tpu_custom_call" | custom-call | flops 1040187392 | bytes 6291456 | tf_op jit(solution)/shard_map/far_pass/pallas_call | solution.py:352
Async XLA Ops:
  1.3 24.6 %all-to-all-start.1 = ((s32[12,1,32]{2,1,0:T(1,128)}), s32[12,1,32]{2,1,0:T(1,128)S(1)}, u32[]{:S(2)}, u32[]{:S(2)}) async-start(s32[12,1,32]{2,1,0:T(1,128)} %broadcast_in_dim.7), calls=%async_computation.1 | async-start | bytes 12288 | tf_op jit(solution)/shard_map/all_to_all | solution.py:377
  25.9 12.3 %copy-start.4 = (s32[12,1,32]{2,1,0:T(1,128)}, s32[12,1,32]{2,1,0:T(1,128)S(1)}, u32[]{:S(2)}) copy-start(s32[12,1,32]{2,1,0:T(1,128)S(1)} %all-to-all-done.1.asked_ref) | copy-start | bytes 4612
  25.9 21.7 %all-to-all-start = ((s32[64,1,8]{2,1,0:T(1,128)}), s32[64,1,8]{2,1,0:T(1,128)S(1)}, u32[]{:S(2)}, u32[]{:S(2)}) async-start(s32[64,1,8]{2,1,0:T(1,128)} %bitcast), calls=%async_computation | async-start | bytes 65536 | tf_op jit(solution)/shard_map/all_to_all | solution.py:377
  47.6 5.2 %copy-start.3 = (s32[64,1,8]{2,1,0:T(1,128)}, s32[64,1,8]{2,1,0:T(1,128)S(1)}, u32[]{:S(2)}) copy-start(s32[64,1,8]{2,1,0:T(1,128)S(1)} %all-to-all-done.asked_ref) | copy-start | bytes 6148
  47.6 18.2 %all-to-all-start.3 = ((bf16[12,32,256]{2,1,0:T(8,128)(2,1)}), bf16[12,32,256]{2,1,0:T(8,128)(2,1)S(1)}, u32[]{:S(2)}, u32[]{:S(2)}) async-start(bf16[12,32,256]{2,1,0:T(8,128)(2,1)} %bitcast.8), calls=%async_computation.3 | async-start | bytes 393216 | tf_op jit(solution)/shard_map/all_to_all | solution.py:377
  65.7 9.1 %copy-start.2 = (bf16[12,32,256]{2,1,0:T(8,128)(2,1)}, bf16[12,32,256]{2,1,0:T(8,128)(2,1)S(1)}, u32[]{:S(2)}) copy-start(bf16[12,32,256]{2,1,0:T(8,128)(2,1)S(1)} %all-to-all-done.3) | copy-start | bytes 589828
  65.7 22.2 %all-to-all-start.2 = ((bf16[64,8,256]{2,1,0:T(8,128)(2,1)}), bf16[64,8,256]{2,1,0:T(8,128)(2,1)S(1)}, u32[]{:S(2)}, u32[]{:S(2)}) async-start(bf16[64,8,256]{2,1,0:T(8,128)(2,1)} %bitcast.6), calls=%async_computation.2 | async-start | bytes 524288 | tf_op jit(solution)/shard_map/all_to_all | solution.py:377
  74.8 13.1 %copy-start = (bf16[8,256,256]{2,1,0:T(8,128)(2,1)S(1)}, bf16[8,256,256]{2,1,0:T(8,128)(2,1)}, u32[]{:S(2)}) copy-start(bf16[8,256,256]{2,1,0:T(8,128)(2,1)} %down_in.1) | copy-start | bytes 3145732
  74.8 13.1 %copy-start.1 = (s32[1168,16]{1,0:T(8,128)S(1)}, s32[1168,16]{1,0:T(8,128)}, u32[]{:S(2)}) copy-start(s32[1168,16]{1,0:T(8,128)} %get-tuple-element.16.refs_2_.pairs_in) | copy-start | bytes 224260

commit v3 on v2

--- a/solution.py
+++ b/solution.py
@@ -5,6 +5,7 @@
 from jax import lax
 from jax.experimental import pallas as pl
 from jax.experimental.pallas import tpu as pltpu
+from jax.sharding import Mesh
 from jax.sharding import PartitionSpec as P
 
 BF16 = jnp.bfloat16
@@ -49,8 +50,8 @@
     return copy
 
 
-def up_kernel(live_ref, source_ref, moments_in, up_in, fine_out, high_out, pairs_out,
-              fine, up, high, pairs, wide, sems):
+def up_kernel(live_ref, source_ref, asks_ref, moments_in, up_in, fine_out, high_out, pairs_out, asks_out,
+              fine, up, high, pairs, wide, square, sems):
     count, size = fine.shape
     middles = count // 8
     get_fine = start(moments_in, fine, sems.at[0])
@@ -63,6 +64,15 @@
             block = jnp.concatenate([block, jnp.zeros((block.shape[0], 128 - there), I32)], axis=1)
         pairs[low : low + there, :] = block.T[:there, :]
     put_pairs = start(pairs, pairs_out, sems.at[2])
+    slots, leaves = asks_ref.shape
+    square[...] = jnp.zeros(square.shape, I32)
+    square[:slots, :leaves] = asks_ref[...]
+    square[...] = square[...].T
+    own = square[pl.ds(0, leaves // 2, stride=2), :]
+    other = square[pl.ds(1, leaves // 2, stride=2), :]
+    asks = own + pltpu.roll(other, slots, 1)
+    for chip in range(leaves // 2):
+        asks_out[chip] = asks[chip : chip + 1, : 2 * slots]
     live = live_ref[0]
     get_fine.wait()
     for m in range(count // TILE):
@@ -94,8 +104,9 @@
         put.wait()
 
 
-def up_pass(live, source, moments, up):
+def up_pass(live, source, asks, moments, up):
     count, size = moments.shape
+    slots, leaves = asks.shape
     offsets, cells = source.shape
     upper = cells - count
     return pl.pallas_call(
@@ -104,61 +115,67 @@
             jax.ShapeDtypeStruct((count, size), BF16),
             jax.ShapeDtypeStruct((upper, size), BF16),
             jax.ShapeDtypeStruct((cells, offsets), I32),
+            jax.ShapeDtypeStruct((leaves // 2, 1, 2 * slots), I32),
         ),
-        in_specs=[SMEM, VMEM, ANY, ANY],
-        out_specs=(ANY, ANY, ANY),
+        in_specs=[SMEM, VMEM, VMEM, ANY, ANY],
+        out_specs=(ANY, ANY, ANY, VMEM),
         scratch_shapes=[
             pltpu.VMEM((count, size), BF16),
             pltpu.VMEM(up.shape, BF16),
             pltpu.VMEM((upper, size), BF16),
             pltpu.VMEM((cells, offsets), I32),
             pltpu.VMEM((2, count, 128), F32),
+            pltpu.VMEM((128, 128), I32),
             pltpu.SemaphoreType.DMA((3,)),
         ],
         compiler_params=PARAMS,
         cost_estimate=cost(count * size * size, 3 << 20),
         name="up_pass",
-    )(live, source, moments, up)
-
-
-def own_kernel(first, low, offsets, asked_ref, *refs):
+    )(live, source, asks, moments, up)
+
+
+def own_kernel(first, offsets, asked_ref, *refs):
     if first:
         fine_in, high_in, pairs_in, ops_in, picked_out, total_out = refs[:6]
         refs = refs[6:]
     else:
-        fine_in, high_in, pairs_in, ops_in, total_in, picked_out, total_out = refs[:7]
-        refs = refs[7:]
+        core_ref, fine_in, high_in, other_in, pairs_in, ops_in, total_in, picked_out, total_out = refs[:9]
+        refs = refs[9:]
     table, pairs, ops, total, moved, wide, picked, sems = refs
     count = total.shape[0]
+    middles = count // 8
     upper = high_in.shape[0]
     steps = len(offsets)
+    end = table.shape[0]
     gets = [
         start(fine_in, table.at[pl.ds(0, count)], sems.at[0]),
-        start(high_in, table.at[pl.ds(count, upper)], sems.at[1]),
-        start(pairs_in, pairs, sems.at[2]),
-        start(ops_in.at[pl.ds(offsets[0], steps)], ops, sems.at[3]),
+        start(pairs_in, pairs, sems.at[1]),
+        start(ops_in.at[pl.ds(offsets[0], steps)], ops, sems.at[2]),
     ]
-    if not first:
-        gets.append(start(total_in, total, sems.at[4]))
-    end = table.shape[0]
-    table[count + upper : end, :] = jnp.zeros((end - count - upper, table.shape[1]), BF16)
+    if first:
+        gets.append(start(high_in.at[pl.ds(0, middles)], table.at[pl.ds(count, middles)], sems.at[3]))
+    else:
+        gets.append(start(high_in, table.at[pl.ds(count, upper)], sems.at[3]))
+        gets.append(start(other_in, table.at[pl.ds(count + upper, upper)], sems.at[4]))
+        gets.append(start(total_in, total, sems.at[5]))
+        used = count + 2 * upper
+        table[used:end, :] = jnp.zeros((end - used, table.shape[1]), BF16)
     peers, unit, slots = asked_ref.shape
     wide[...] = jnp.zeros(wide.shape, I32)
     for p in range(peers):
         wide[p : p + 1, :slots] = asked_ref[p]
-    asked = wide[...].T - low
+    asked = wide[...].T[:slots, :]
+    if first:
+        low = 0
+    else:
+        low = count
+        here = lax.broadcasted_iota(I32, asked.shape, 0) // (slots // 2) == core_ref[0]
+        asked = asked - count + jnp.where(here, 0, upper)
     for get in gets:
         get.wait()
-    span = end - low
-    if slots % 16 == 0:
-        hot = jnp.concatenate(
-            [one_hot([asked[:slots, p : p + 1]], 0, span) for p in range(peers)], axis=0
-        )
-    else:
-        lane = lax.broadcasted_iota(I32, (slots, span), 1)
-        hot = jnp.concatenate(
-            [jnp.where(asked[:slots, p : p + 1] == lane, 1.0, 0.0) for p in range(peers)], axis=0
-        ).astype(BF16)
+    hot = jnp.concatenate(
+        [one_hot([asked[:, p : p + 1]], 0, end - low) for p in range(peers)], axis=0
+    )
     picked[...] = dot(hot, table[low:end, :]).astype(BF16)
     puts = [start(picked, picked_out, sems.at[0])]
     for n, o in enumerate(offsets):
@@ -174,29 +191,37 @@
         put.wait()
 
 
-def own_pass(low, asked, fine, high, pairs, ops, offsets, total):
+def own_pass(asked, fine, high, pairs, ops, offsets, others):
     count, size = fine.shape
-    first = total is None
-    args = (asked, fine, high, pairs, ops) + (() if first else (total,))
+    first = others is None
+    if first:
+        args = (asked, fine, high, pairs, ops)
+        specs = [VMEM] + [ANY] * 4
+        rows = count + count // 8
+    else:
+        core, other, total = others
+        args = (asked, core, fine, high, other, pairs, ops, total)
+        specs = [VMEM, SMEM] + [ANY] * 6
+        rows = count + 384
     steps = len(offsets)
     replies = asked.shape[0] * asked.shape[2]
     return pl.pallas_call(
-        functools.partial(own_kernel, first, low, offsets),
+        functools.partial(own_kernel, first, offsets),
         out_shape=(
             jax.ShapeDtypeStruct((replies, size), BF16),
             jax.ShapeDtypeStruct((count, size), F32),
         ),
-        in_specs=[VMEM] + [ANY] * (len(args) - 1),
+        in_specs=specs,
         out_specs=(ANY, ANY),
         scratch_shapes=[
-            pltpu.VMEM((count + 256, size), BF16),
+            pltpu.VMEM((rows, size), BF16),
             pltpu.VMEM(pairs.shape, I32),
             pltpu.VMEM((steps, size, size), BF16),
             pltpu.VMEM((count, size), F32),
             pltpu.VMEM((2, count, size), BF16),
             pltpu.VMEM((128, 128), I32),
             pltpu.VMEM((replies, size), BF16),
-            pltpu.SemaphoreType.DMA((5,)),
+            pltpu.SemaphoreType.DMA((6,)),
         ],
         compiler_params=PARAMS,
         cost_estimate=cost(steps * count * size * (size + count), 4 << 20),
@@ -390,14 +415,19 @@
     early = tuple(range(EARLY))
     late = tuple(range(EARLY, offsets))
     near_asked = exchange(near_requests[:, None, :], "grp")
-    fine, high, pairs = up_pass(live_fine, pair_source, moments, child_up)
-    far_asked = exchange(after(far_requests, high)[:, None, :], "leaf")
-    replies, total = own_pass(0, near_asked, fine, high, pairs, offset_ops, early, None)
+    fine, high, pairs, asks = up_pass(
+        live_fine, pair_source, far_requests.T, moments, child_up
+    )
+    other = lax.ppermute(high, "core", [(0, 1), (1, 0)])
+    far_asked = exchange(after(asks, high), "chip")
+    replies, total = own_pass(near_asked, fine, high, pairs, offset_ops, early, None)
     near_tiles = exchange(replies.reshape(-1, slots, size), "grp").reshape(-1, size)
+    core = lax.axis_index("core").reshape(1)
     replies, total = own_pass(
-        fine_count, far_asked, fine, high, pairs, offset_ops, late, total
-    )
-    far_tiles = exchange(replies.reshape(far_requests.shape + (size,)), "leaf").reshape(-1, size)
+        far_asked, fine, high, pairs, offset_ops, late, (core, other, total)
+    )
+    far_tiles = exchange(replies.reshape(-1, 2 * far_requests.shape[1], size), "chip")
+    far_tiles = far_tiles.reshape(-1, size)
     sums = near_pass(
         cells, (slots * 3 // 4, slots), near_tiles, high, pairs, offset_ops, total
     )
@@ -406,7 +436,9 @@
 
 
 def solution(mesh):
-    axes = ("leaf", "grp")
+    leaf, grp = mesh.devices.shape
+    axes = ("chip", "core", "grp")
+    split = Mesh(mesh.devices.reshape(leaf // 2, 2, grp), axes)
     in_specs = (
         P(axes, None),
         P(axes),
@@ -418,5 +450,5 @@
         P(),
     )
     return jax.shard_map(
-        body, mesh=mesh, in_specs=in_specs, out_specs=P(axes, None), check_vma=False
-    )
+        body, mesh=split, in_specs=in_specs, out_specs=P(axes, None), check_vma=False
+    )

time: 92.9 us -> 90.1 us (0.970)
  the two profiles are of different devices: /device:TPU:1 before, /device:TPU:64 now
where the time goes in v3:
time: 90.1 us; the launch traced here: 89.4 us
  starting transfers between devices  41.5 us (46%)
  Pallas kernels  35.1 us (39%)
  waiting for transfers between devices  9.96 us (11%)
  local copies, waits for them, and re-layouts  1.93 us (2%)
  between operations  0.97 us (1%)
    all_to_all x4, starting transfers between devices, exchange(): return lax.all_to_all(rows, axis, split_axis=0, concat_axis=0, tiled=True)  39.5 us
    pallas_call x2, Pallas kernels, own_pass(): pl.pallas_call(functools.partial(own_kernel, first, offsets), out_shape=(...  19.5 us
    all_to_all x4, waiting for transfers between devices, exchange(): return lax.all_to_all(rows, axis, split_axis=0, concat_axis=0, tiled=True)  9.95 us
    pallas_call x1, Pallas kernels, near_pass(): pl.pallas_call(functools.partial(near_kernel, base, asked), out_shape=jax...  7.15 us
    pallas_call x1, Pallas kernels, up_pass(): pl.pallas_call(up_kernel, out_shape=(jax.ShapeDtypeStruct((count, size),...  4.4 us
    pallas_call x1, Pallas kernels, far_pass(): pl.pallas_call(functools.partial(far_kernel, base), out_shape=jax.ShapeDt...  4.08 us
    ppermute x1, starting transfers between devices, body(): other = lax.ppermute(high, 'core', [(0, 1), (1, 0)])  1.92 us
  transfers between devices with their start and end apart: 5, of which 3 were waited for; matrix products, arithmetic and copies ran while one was open for 0% of the time, Pallas kernels for 35%

profile of v3, /device:TPU:64, one launch (start us, length us, event | category | flops | bytes accessed | tf_op | source)
XLA Modules:
  0.0 89.4 jit_solution(8519143934572478024)
XLA Ops:
  0.0 1.3 %broadcast_in_dim.3 = s32[12,1,32]{2,1,0:T(1,128)} reshape(s32[12,32]{1,0:T(8,128)} %param.10) | data formatting | bytes 3072 | tf_op jit(solution)/shard_map/broadcast_in_dim | solution.py:417
  1.3 14.8 %all-to-all-start.1 = ((s32[12,1,32]{2,1,0:T(1,128)}), s32[12,1,32]{2,1,0:T(1,128)S(1)}, u32[]{:S(2)}, u32[]{:S(2)}) async-start(s32[12,1,32]{2,1,0:T(1,128)} %broadcast_in_dim.3), calls=%async_computation.1 | async-start | bytes 12288 | tf_op jit(solution)/shard_map/all_to_all | solution.py:402
  16.7 4.4 %up_pass.1 = (bf16[1024,256]{1,0:T(8,128)(2,1)}, bf16[144,256]{1,0:T(8,128)(2,1)}, s32[1168,16]{1,0:T(8,128)}, s32[32,1,16]{2,1,0:T(1,128)}) custom-call(s32[1]{0:T(128)S(6)} %copy.9.live_ref, s32[16,1168]{1,0:T(8,128)} %source_ref.1, s32[8,64]{1,0:T(8,128)} %bitcast.10, bf16[1024,256]{1,0:T(8,128)(2,1)} %moments_in.1, bf16[8,256,256]{2,1,0:T(8,128)(2,1)} %up_in.1), custom_call_target="tpu_custom_call" | custom-call | flops 134217728 | bytes 3145728 | tf_op jit(solution)/shard_map/up_pass/pallas_call | solution.py:112
  21.1 1.9 %collective-permute-start = (bf16[144,256]{1,0:T(8,128)(2,1)}, bf16[144,256]{1,0:T(8,128)(2,1)S(1)}, u32[]{:S(2)}, u32[]{:S(2)}) collective-permute-start(bf16[144,256]{1,0:T(8,128)(2,1)} %get-tuple-element.15.refs_1_.refs_2_.high_in), channel_id=1, source_target_pairs={{0,12},{12,0},{1,13},{13,1},{2,14},{14,2},{3,15},{15,3},{4,16},{16... | collective-permute-start | bytes 221192 | tf_op jit(solution)/shard_map/ppermute | solution.py:421
  23.1 1.6 %all-to-all-done.1.asked_ref = s32[12,1,32]{2,1,0:T(1,128)S(1)} async-done(((s32[12,1,32]{2,1,0:T(1,128)}), s32[12,1,32]{2,1,0:T(1,128)S(1)}, u32[]{:S(2)}, u32[]{:S(2)}) %all-to-all-start.1) | async-done | bytes 1568 | tf_op jit(solution)/shard_map/all_to_all | solution.py:402
  24.7 0.0 copy-start.4
  24.7 10.0 %all-to-all-start = ((s32[32,1,16]{2,1,0:T(1,128)}), s32[32,1,16]{2,1,0:T(1,128)S(1)}, u32[]{:S(2)}, u32[]{:S(2)}) async-start(s32[32,1,16]{2,1,0:T(1,128)} %get-tuple-element.16), calls=%async_computation | async-start | bytes 32768 | tf_op jit(solution)/shard_map/all_to_all | solution.py:402
  34.7 0.0 copy-done.4
  34.7 6.5 %own_pass.2 = (bf16[384,256]{1,0:T(8,128)(2,1)}, f32[1024,256]{1,0:T(8,128)}) custom-call(s32[12,1,32]{2,1,0:T(1,128)} %copy-done.4, bf16[1024,256]{1,0:T(8,128)(2,1)} %get-tuple-element.17.refs_0_.refs_1_, bf16[144,256]{1,0:T(8,128)(2,1)} %get-tuple-element.15.refs_1_.refs_2_.high_in, s32[1168,16]{1,0:T(8,128)} %get-tuple-element.18.refs_2_.refs_4_.pairs_in, ...), custom_call_target="tpu_custom_call" | custom-call | flops 2684354560 | bytes 4194304 | tf_op jit(solution)/shard_map/own_pass/pallas_call | solution.py:208
  41.2 3.2 %all-to-all-done.asked_ref = s32[32,1,16]{2,1,0:T(1,128)S(1)} async-done(((s32[32,1,16]{2,1,0:T(1,128)}), s32[32,1,16]{2,1,0:T(1,128)S(1)}, u32[]{:S(2)}, u32[]{:S(2)}) %all-to-all-start) | async-done | bytes 2080 | tf_op jit(solution)/shard_map/all_to_all | solution.py:402
  44.4 0.0 copy-start.3
  44.4 8.0 %all-to-all-start.3 = ((bf16[12,32,256]{2,1,0:T(8,128)(2,1)}), bf16[12,32,256]{2,1,0:T(8,128)(2,1)S(1)}, u32[]{:S(2)}, u32[]{:S(2)}) async-start(bf16[12,32,256]{2,1,0:T(8,128)(2,1)} %bitcast.9), calls=%async_computation.3 | async-start | bytes 393216 | tf_op jit(solution)/shard_map/all_to_all | solution.py:402
  52.4 0.0 collective-permute-done.refs_3_
  52.4 0.0 copy-start.5
  52.4 0.0 copy-done.3
  52.4 0.6 copy-done.5
  53.0 13.0 %own_pass.3 = (bf16[512,256]{1,0:T(8,128)(2,1)}, f32[1024,256]{1,0:T(8,128)}) custom-call(s32[32,1,16]{2,1,0:T(1,128)} %copy-done.3, s32[1]{0:T(128)} %bitcast.1.refs_0_, bf16[1024,256]{1,0:T(8,128)(2,1)} %get-tuple-element.17.refs_0_.refs_1_, bf16[144,256]{1,0:T(8,128)(2,1)} %get-tuple-element.15.refs_1_.refs_2_.high_in, bf16[144,256]{1,0:T(8,128)(2,1)} %copy-done.5, ...), custom_call_target="tpu_custom_call" | custom-call | flops 8053063680 | bytes 4194304 | tf_op jit(solution)/shard_map/own_pass/pallas_call | solution.py:208
  66.1 0.0 all-to-all-done.3
  66.1 0.0 copy-start.2
  66.1 6.8 %all-to-all-start.2 = ((bf16[32,16,256]{2,1,0:T(8,128)(2,1)}), bf16[32,16,256]{2,1,0:T(8,128)(2,1)S(1)}, u32[]{:S(2)}, u32[]{:S(2)}) async-start(bf16[32,16,256]{2,1,0:T(8,128)(2,1)} %bitcast.7), calls=%async_computation.2 | async-start | bytes 524288 | tf_op jit(solution)/shard_map/all_to_all | solution.py:402
  72.9 0.0 copy-done.2
  72.9 0.0 copy-start
  72.9 0.0 copy-start.1
  72.9 7.2 %near_pass.1.sums_in = f32[1152,256]{1,0:T(8,128)} custom-call(bf16[384,256]{1,0:T(8,128)(2,1)} %bitcast.8, bf16[144,256]{1,0:T(8,128)(2,1)} %get-tuple-element.15.refs_1_.refs_2_.high_in, s32[1168,16]{1,0:T(8,128)} %get-tuple-element.18.refs_2_.refs_4_.pairs_in, bf16[16,256,256]{2,1,0:T(8,128)(2,1)} %ops_in.3, f32[1024,256]{1,0:T(8,128)} %get-tuple-element.22.total_in), custom_call_target="tpu_custom_call" | custom-call | flops 3825205248 | bytes 6291456 | tf_op jit(solution)/shard_map/near_pass/pallas_call | solution.py:301
  80.1 5.1 %all-to-all-done.2 = bf16[32,16,256]{2,1,0:T(8,128)(2,1)S(1)} async-done(((bf16[32,16,256]{2,1,0:T(8,128)(2,1)}), bf16[32,16,256]{2,1,0:T(8,128)(2,1)S(1)}, u32[]{:S(2)}, u32[]{:S(2)}) %all-to-all-start.2) | async-done | bytes 262176 | tf_op jit(solution)/shard_map/all_to_all | solution.py:402
  85.2 0.0 copy-done
  85.2 0.0 copy-done.1
  85.2 4.1 %far_pass.1 = bf16[1024,256]{1,0:T(8,128)(2,1)} custom-call(s32[1]{0:T(128)S(6)} %copy.9.live_ref, bf16[512,256]{1,0:T(8,128)(2,1)S(1)} %bitcast.6, s32[1168,16]{1,0:T(8,128)S(1)} %copy-done.1, bf16[16,256,256]{2,1,0:T(8,128)(2,1)} %ops_in.3, bf16[8,256,256]{2,1,0:T(8,128)(2,1)S(1)} %copy-done, f32[1152,256]{1,0:T(8,128)} %near_pass.1.sums_in), custom_call_target="tpu_custom_call" | custom-call | flops 1040187392 | bytes 6291456 | tf_op jit(solution)/shard_map/far_pass/pallas_call | solution.py:377
Async XLA Ops:
  1.3 23.4 %all-to-all-start.1 = ((s32[12,1,32]{2,1,0:T(1,128)}), s32[12,1,32]{2,1,0:T(1,128)S(1)}, u32[]{:S(2)}, u32[]{:S(2)}) async-start(s32[12,1,32]{2,1,0:T(1,128)} %broadcast_in_dim.3), calls=%async_computation.1 | async-start | bytes 12288 | tf_op jit(solution)/shard_map/all_to_all | solution.py:402
  21.1 31.3 %collective-permute-start = (bf16[144,256]{1,0:T(8,128)(2,1)}, bf16[144,256]{1,0:T(8,128)(2,1)S(1)}, u32[]{:S(2)}, u32[]{:S(2)}) collective-permute-start(bf16[144,256]{1,0:T(8,128)(2,1)} %get-tuple-element.15.refs_1_.refs_2_.high_in), channel_id=1, source_target_pairs={{0,12},{12,0},{1,13},{13,1},{2,14},{14,2},{3,15},{15,3},{4,16},{16... | collective-permute-start | bytes 221192 | tf_op jit(solution)/shard_map/ppermute | solution.py:421
  24.7 10.0 %copy-start.4 = (s32[12,1,32]{2,1,0:T(1,128)}, s32[12,1,32]{2,1,0:T(1,128)S(1)}, u32[]{:S(2)}) copy-start(s32[12,1,32]{2,1,0:T(1,128)S(1)} %all-to-all-done.1.asked_ref) | copy-start | bytes 4612
  24.7 19.7 %all-to-all-start = ((s32[32,1,16]{2,1,0:T(1,128)}), s32[32,1,16]{2,1,0:T(1,128)S(1)}, u32[]{:S(2)}, u32[]{:S(2)}) async-start(s32[32,1,16]{2,1,0:T(1,128)} %get-tuple-element.16), calls=%async_computation | async-start | bytes 32768 | tf_op jit(solution)/shard_map/all_to_all | solution.py:402
  44.4 8.0 %copy-start.3 = (s32[32,1,16]{2,1,0:T(1,128)}, s32[32,1,16]{2,1,0:T(1,128)S(1)}, u32[]{:S(2)}) copy-start(s32[32,1,16]{2,1,0:T(1,128)S(1)} %all-to-all-done.asked_ref) | copy-start | bytes 6148
  44.4 21.7 %all-to-all-start.3 = ((bf16[12,32,256]{2,1,0:T(8,128)(2,1)}), bf16[12,32,256]{2,1,0:T(8,128)(2,1)S(1)}, u32[]{:S(2)}, u32[]{:S(2)}) async-start(bf16[12,32,256]{2,1,0:T(8,128)(2,1)} %bitcast.9), calls=%async_computation.3 | async-start | bytes 393216 | tf_op jit(solution)/shard_map/all_to_all | solution.py:402
  52.4 0.6 copy-start.5
  66.1 6.8 %copy-start.2 = (bf16[12,32,256]{2,1,0:T(8,128)(2,1)}, bf16[12,32,256]{2,1,0:T(8,128)(2,1)S(1)}, u32[]{:S(2)}) copy-start(bf16[12,32,256]{2,1,0:T(8,128)(2,1)S(1)} %all-to-all-done.3) | copy-start | bytes 589828
  66.1 19.1 %all-to-all-start.2 = ((bf16[32,16,256]{2,1,0:T(8,128)(2,1)}), bf16[32,16,256]{2,1,0:T(8,128)(2,1)S(1)}, u32[]{:S(2)}, u32[]{:S(2)}) async-start(bf16[32,16,256]{2,1,0:T(8,128)(2,1)} %bitcast.7), calls=%async_computation.2 | async-start | bytes 524288 | tf_op jit(solution)/shard_map/all_to_all | solution.py:402
  72.9 12.3 %copy-start = (bf16[8,256,256]{2,1,0:T(8,128)(2,1)S(1)}, bf16[8,256,256]{2,1,0:T(8,128)(2,1)}, u32[]{:S(2)}) copy-start(bf16[8,256,256]{2,1,0:T(8,128)(2,1)} %down_in.1) | copy-start | bytes 3145732
  72.9 12.3 %copy-start.1 = (s32[1168,16]{1,0:T(8,128)S(1)}, s32[1168,16]{1,0:T(8,128)}, u32[]{:S(2)}) copy-start(s32[1168,16]{1,0:T(8,128)} %get-tuple-element.18.refs_2_.refs_4_.pairs_in) | copy-start | bytes 224260

commit v4 on v3

--- a/solution.py
+++ b/solution.py
@@ -13,10 +13,11 @@
 I32 = jnp.int32
 TILE = 256
 EARLY = 4
+LAST = 14
 ANY = pl.BlockSpec(memory_space=pl.ANY)
 VMEM = pl.BlockSpec(memory_space=pltpu.VMEM)
 SMEM = pl.BlockSpec(memory_space=pltpu.SMEM)
-TIGHT = pltpu.CompilerParams(vmem_limit_bytes=53000 << 10)
+TIGHT = pltpu.CompilerParams(vmem_limit_bytes=51000 << 10)
 PARAMS = pltpu.CompilerParams(vmem_limit_bytes=56 << 20)
 
 
@@ -50,7 +51,7 @@
     return copy
 
 
-def up_kernel(live_ref, source_ref, asks_ref, moments_in, up_in, fine_out, high_out, pairs_out, asks_out,
+def up_kernel(live_ref, source_ref, asks_ref, moments_in, up_in, fine_out, high_out, pairs_out, upper_out, asks_out,
               fine, up, high, pairs, wide, square, sems):
     count, size = fine.shape
     middles = count // 8
@@ -64,6 +65,7 @@
             block = jnp.concatenate([block, jnp.zeros((block.shape[0], 128 - there), I32)], axis=1)
         pairs[low : low + there, :] = block.T[:there, :]
     put_pairs = start(pairs, pairs_out, sems.at[2])
+    upper_out[...] = pairs[count:, :]
     slots, leaves = asks_ref.shape
     square[...] = jnp.zeros(square.shape, I32)
     square[:slots, :leaves] = asks_ref[...]
@@ -115,10 +117,11 @@
             jax.ShapeDtypeStruct((count, size), BF16),
             jax.ShapeDtypeStruct((upper, size), BF16),
             jax.ShapeDtypeStruct((cells, offsets), I32),
+            jax.ShapeDtypeStruct((upper, offsets), I32),
             jax.ShapeDtypeStruct((leaves // 2, 1, 2 * slots), I32),
         ),
         in_specs=[SMEM, VMEM, VMEM, ANY, ANY],
-        out_specs=(ANY, ANY, ANY, VMEM),
+        out_specs=(ANY, ANY, ANY, VMEM, VMEM),
         scratch_shapes=[
             pltpu.VMEM((count, size), BF16),
             pltpu.VMEM(up.shape, BF16),
@@ -132,6 +135,18 @@
         cost_estimate=cost(count * size * size, 3 << 20),
         name="up_pass",
     )(live, source, asks, moments, up)
+
+
+def add_own(offsets, fine, pairs, ops, low, moved, total, fresh):
+    count = fine.shape[0]
+    for n, o in enumerate(offsets):
+        moved[n % 2] = dot(fine[...], ops[o - low]).astype(BF16)
+        for m in range(count // TILE):
+            rows = slice(m * TILE, (m + 1) * TILE)
+            part = dot(one_hot([pairs[rows, o : o + 1]], 0, count), moved[n % 2])
+            if n > 0 or not fresh:
+                part = part + total[rows, :]
+            total[rows, :] = part
 
 
 def own_kernel(first, offsets, asked_ref, *refs):
@@ -178,14 +193,8 @@
     )
     picked[...] = dot(hot, table[low:end, :]).astype(BF16)
     puts = [start(picked, picked_out, sems.at[0])]
-    for n, o in enumerate(offsets):
-        moved[n % 2] = dot(table[:count, :], ops[n]).astype(BF16)
-        for m in range(count // TILE):
-            rows = slice(m * TILE, (m + 1) * TILE)
-            part = dot(one_hot([pairs[rows, o : o + 1]], 0, count), moved[n % 2])
-            if n > 0 or not first:
-                part = part + total[rows, :]
-            total[rows, :] = part
+    fine = table.at[pl.ds(0, count)]
+    add_own(offsets, fine, pairs, ops, offsets[0], moved, total, first)
     puts.append(start(total, total_out, sems.at[1]))
     for put in puts:
         put.wait()
@@ -229,8 +238,8 @@
     )(*args)
 
 
-def near_kernel(base, asked, near_in, high_in, pairs_in, ops_in, total_in, sums_out,
-                near, table, pairs, ops, total, moved, picked, sems):
+def near_kernel(base, asked, own, near_in, fine_in, high_in, pairs_in, ops_in, total_in, sums_out,
+                near, fine, table, pairs, ops, total, moved, own_moved, picked, sems):
     fine_slots, slots = asked
     groups = near.shape[0] // slots
     mid_slots = slots - fine_slots
@@ -241,6 +250,7 @@
     near_mid = groups * mid_slots
     gets = [
         start(near_in, near, sems.at[0]),
+        start(fine_in, fine, sems.at[5]),
         start(ops_in, ops, sems.at[1]),
         start(pairs_in, pairs, sems.at[2]),
         start(high_in.at[pl.ds(0, middles)], table.at[pl.ds(0, middles)], sems.at[3]),
@@ -268,6 +278,7 @@
                 pieces.append(one_hot([place[:, o : o + 1] for o in touched], low, 128))
             part = part + dot(jnp.concatenate(pieces, axis=1), moved[first : first + width, :])
         total[rows, :] = part
+    add_own(own, fine, pairs, ops, 0, own_moved, total, False)
     fines_in = pl.ds(0, count)
     puts = [start(total.at[fines_in], sums_out.at[fines_in], sems.at[0])]
     table[middles : middles + near_mid, :] = jnp.concatenate(
@@ -292,55 +303,51 @@
         put.wait()
 
 
-def near_pass(base, asked, near, high, pairs, ops, total):
+def near_pass(base, asked, own, near, fine, high, pairs, ops, total):
     count, size = total.shape
     middles = count // 8
     offsets = ops.shape[0]
     near_fine = near.shape[0] // asked[1] * asked[0]
     macs = offsets * near_fine * size * (size + count) + 3 * offsets * middles * size * size
     return pl.pallas_call(
-        functools.partial(near_kernel, base, asked),
-        out_shape=jax.ShapeDtypeStruct((count + middles, size), F32),
-        in_specs=[ANY] * 5,
+        functools.partial(near_kernel, base, asked, own),
+        out_shape=jax.ShapeDtypeStruct((8 * count, size), F32),
+        in_specs=[ANY] * 6,
         out_specs=ANY,
         scratch_shapes=[
             pltpu.VMEM(near.shape, BF16),
+            pltpu.VMEM((count, size), BF16),
             pltpu.VMEM((256, size), BF16),
             pltpu.VMEM(pairs.shape, I32),
             pltpu.VMEM(ops.shape, BF16),
             pltpu.VMEM((count + middles, size), F32),
             pltpu.VMEM((offsets * near_fine, size), BF16),
+            pltpu.VMEM((2, count, size), BF16),
             pltpu.VMEM((offsets, middles, size), BF16),
-            pltpu.SemaphoreType.DMA((5,)),
+            pltpu.SemaphoreType.DMA((6,)),
         ],
         compiler_params=PARAMS,
         cost_estimate=cost(macs, 6 << 20),
         name="near_pass",
-    )(near, high, pairs, ops, total)
-
-
-def far_kernel(base, live_ref, far_ref, pairs_in, ops_in, down_in, sums_in, out_out,
-               pairs, ops, down, mid, total, out, picked, mid_wide, fine_wide, sems, out_sems):
+    )(near, fine, high, pairs, ops, total)
+
+
+def far_kernel(base, live_ref, far_ref, pairs, ops, down, sums_in, out_out,
+               mid, total, out, picked, mid_wide, fine_wide, sems, out_sems):
     count = total.shape[0]
     middles = mid.shape[0]
     cells = pairs.shape[0]
     offsets = ops.shape[0]
-    get_pairs = start(pairs_in.at[pl.ds(count, cells)], pairs, sems.at[0])
-    get_ops = start(ops_in, ops, sems.at[1])
-    get_mid = start(sums_in.at[pl.ds(count, middles)], mid, sems.at[2])
-    get_down = start(down_in, down, sems.at[3])
-    get_total = start(sums_in.at[pl.ds(0, count)], total, sems.at[4])
-    get_pairs.wait()
+    get_mid = start(sums_in.at[pl.ds(count, middles)], mid, sems.at[0])
+    get_total = start(sums_in.at[pl.ds(0, count)], total, sems.at[1])
     place = pairs[...] - base
     for o in range(offsets):
         hot = one_hot([place[:, o : o + 1]], 0, far_ref.shape[0])
         picked[o] = dot(hot, far_ref[...]).astype(BF16)
-    get_ops.wait()
     field = dot(picked[0], ops[0])
     for o in range(1, offsets):
         field = field + dot(picked[o], ops[o])
     get_mid.wait()
-    get_down.wait()
     coarse = field[middles:, :].astype(BF16)
     for k in range(8):
         rows = pl.ds(k, cells - middles, stride=8)
@@ -369,27 +376,24 @@
 
 def far_pass(base, live, far, pairs, ops, down, sums):
     size = sums.shape[1]
-    count = sums.shape[0] // 9 * 8
-    middles = count // 8
-    cells = pairs.shape[0] - count
+    cells = pairs.shape[0]
+    middles = cells // 9 * 8
+    count = middles * 8
     offsets = ops.shape[0]
     macs = offsets * cells * size * (far.shape[0] + size) + count * size * size
     return pl.pallas_call(
         functools.partial(far_kernel, base),
         out_shape=jax.ShapeDtypeStruct((count, size), BF16),
-        in_specs=[SMEM, VMEM] + [ANY] * 4,
+        in_specs=[SMEM] + [VMEM] * 4 + [ANY],
         out_specs=ANY,
         scratch_shapes=[
-            pltpu.VMEM((cells, pairs.shape[1]), I32),
-            pltpu.VMEM(ops.shape, BF16),
-            pltpu.VMEM(down.shape, BF16),
             pltpu.VMEM((middles, size), F32),
             pltpu.VMEM((count, size), F32),
             pltpu.VMEM((count, size), BF16),
             pltpu.VMEM((offsets, cells, size), BF16),
             pltpu.VMEM((2, middles, 128), F32),
             pltpu.VMEM((2, count, 128), F32),
-            pltpu.SemaphoreType.DMA((5,)),
+            pltpu.SemaphoreType.DMA((2,)),
             pltpu.SemaphoreType.DMA((count // TILE,)),
         ],
         compiler_params=TIGHT,
@@ -413,9 +417,10 @@
     offsets, cells = pair_source.shape
     slots = near_requests.shape[1]
     early = tuple(range(EARLY))
-    late = tuple(range(EARLY, offsets))
+    late = tuple(range(EARLY, LAST))
+    last = tuple(range(LAST, offsets))
     near_asked = exchange(near_requests[:, None, :], "grp")
-    fine, high, pairs, asks = up_pass(
+    fine, high, pairs, upper_pairs, asks = up_pass(
         live_fine, pair_source, far_requests.T, moments, child_up
     )
     other = lax.ppermute(high, "core", [(0, 1), (1, 0)])
@@ -429,10 +434,10 @@
     far_tiles = exchange(replies.reshape(-1, 2 * far_requests.shape[1], size), "chip")
     far_tiles = far_tiles.reshape(-1, size)
     sums = near_pass(
-        cells, (slots * 3 // 4, slots), near_tiles, high, pairs, offset_ops, total
+        cells, (slots * 3 // 4, slots), last, near_tiles, fine, high, pairs, offset_ops, total
     )
     far_base = cells + near_tiles.shape[0]
-    return far_pass(far_base, live_fine, far_tiles, pairs, offset_ops, child_down, sums)
+    return far_pass(far_base, live_fine, far_tiles, upper_pairs, offset_ops, child_down, sums)
 
 
 def solution(mesh):

time: 90.1 us -> 89.7 us (level)
  Pallas kernels: 35.1 us -> 34.1 us
    pallas_call x1, Pallas kernels: 7.15 us -> 8.67 us  [near_pass(): pl.pallas_call(functools.partial(near_kernel, base, asked, own), out_shap...]
    pallas_call x2, Pallas kernels: 19.5 us -> 18 us  [own_pass(): pl.pallas_call(functools.partial(own_kernel, first, offsets), out_shape=(...]
    pallas_call x1, Pallas kernels: 4.08 us -> 3.08 us  [far_pass(): pl.pallas_call(functools.partial(far_kernel, base), out_shape=jax.ShapeDt...]
  transfers between devices with their start and end apart: 5 -> 5, of which waited for: 3 -> 4; matrix products, arithmetic and copies ran while one was open for 0% -> 0% of each run, Pallas kernels for 35% -> 35%
where the time goes in v4:
time: 89.7 us; the launch traced here: 89.1 us
  starting transfers between devices  42.1 us (47%)
  Pallas kernels  34.1 us (38%)
  waiting for transfers between devices  9.32 us (10%)
  local copies, waits for them, and re-layouts  2.62 us (3%)
  between operations  0.94 us (1%)
    all_to_all x4, starting transfers between devices, exchange(): return lax.all_to_all(rows, axis, split_axis=0, concat_axis=0, tiled=True)  40.2 us
    pallas_call x2, Pallas kernels, own_pass(): pl.pallas_call(functools.partial(own_kernel, first, offsets), out_shape=(...  18 us
    all_to_all x4, waiting for transfers between devices, exchange(): return lax.all_to_all(rows, axis, split_axis=0, concat_axis=0, tiled=True)  9.31 us
    pallas_call x1, Pallas kernels, near_pass(): pl.pallas_call(functools.partial(near_kernel, base, asked, own), out_shap...  8.67 us
    pallas_call x1, Pallas kernels, up_pass(): pl.pallas_call(up_kernel, out_shape=(jax.ShapeDtypeStruct((count, size),...  4.41 us
    pallas_call x1, Pallas kernels, far_pass(): pl.pallas_call(functools.partial(far_kernel, base), out_shape=jax.ShapeDt...  3.08 us
    ppermute x1, starting transfers between devices, body(): other = lax.ppermute(high, 'core', [(0, 1), (1, 0)])  1.92 us
  transfers between devices with their start and end apart: 5, of which 4 were waited for; matrix products, arithmetic and copies ran while one was open for 0% of the time, Pallas kernels for 35%

profile of v4, /device:TPU:64, one launch (start us, length us, event | category | flops | bytes accessed | tf_op | source)
XLA Modules:
  0.0 89.1 jit_solution(6513142280326354256)
XLA Ops:
  0.0 1.3 %broadcast_in_dim.3 = s32[12,1,32]{2,1,0:T(1,128)} reshape(s32[12,32]{1,0:T(8,128)} %param.10) | data formatting | bytes 3072 | tf_op jit(solution)/shard_map/broadcast_in_dim | solution.py:422
  1.3 14.8 %all-to-all-start.1 = ((s32[12,1,32]{2,1,0:T(1,128)}), s32[12,1,32]{2,1,0:T(1,128)S(1)}, u32[]{:S(2)}, u32[]{:S(2)}) async-start(s32[12,1,32]{2,1,0:T(1,128)} %broadcast_in_dim.3), calls=%async_computation.1 | async-start | bytes 12288 | tf_op jit(solution)/shard_map/all_to_all | solution.py:406
  16.7 4.4 %up_pass.1 = (bf16[1024,256]{1,0:T(8,128)(2,1)}, bf16[144,256]{1,0:T(8,128)(2,1)}, s32[1168,16]{1,0:T(8,128)}, s32[144,16]{1,0:T(8,128)}, s32[32,1,16]{2,1,0:T(1,128)}) custom-call(s32[1]{0:T(128)S(6)} %copy.9.live_ref, s32[16,1168]{1,0:T(8,128)} %source_ref.1, s32[8,64]{1,0:T(8,128)} %bitcast.10, bf16[1024,256]{1,0:T(8,128)(2,1)} %moments_in.1, ...), custom_call_target="tpu_custom_call" | custom-call | flops 134217728 | bytes 3145728 | tf_op jit(solution)/shard_map/up_pass/pallas_call | solution.py:114
  21.1 1.9 %collective-permute-start = (bf16[144,256]{1,0:T(8,128)(2,1)}, bf16[144,256]{1,0:T(8,128)(2,1)S(1)}, u32[]{:S(2)}, u32[]{:S(2)}) collective-permute-start(bf16[144,256]{1,0:T(8,128)(2,1)} %get-tuple-element.16.refs_1_.refs_2_.high_in), channel_id=1, source_target_pairs={{0,12},{12,0},{1,13},{13,1},{2,14},{14,2},{3,15},{15,3},{4,16},{16... | collective-permute-start | bytes 221192 | tf_op jit(solution)/shard_map/ppermute | solution.py:426
  23.1 1.6 %all-to-all-done.1.asked_ref = s32[12,1,32]{2,1,0:T(1,128)S(1)} async-done(((s32[12,1,32]{2,1,0:T(1,128)}), s32[12,1,32]{2,1,0:T(1,128)S(1)}, u32[]{:S(2)}, u32[]{:S(2)}) %all-to-all-start.1) | async-done | bytes 1568 | tf_op jit(solution)/shard_map/all_to_all | solution.py:406
  24.7 0.0 copy-start.5
  24.7 10.0 %all-to-all-start = ((s32[32,1,16]{2,1,0:T(1,128)}), s32[32,1,16]{2,1,0:T(1,128)S(1)}, u32[]{:S(2)}, u32[]{:S(2)}) async-start(s32[32,1,16]{2,1,0:T(1,128)} %get-tuple-element.17), calls=%async_computation | async-start | bytes 32768 | tf_op jit(solution)/shard_map/all_to_all | solution.py:406
  34.7 0.0 copy-done.5
  34.7 6.4 %own_pass.2 = (bf16[384,256]{1,0:T(8,128)(2,1)}, f32[1024,256]{1,0:T(8,128)}) custom-call(s32[12,1,32]{2,1,0:T(1,128)} %copy-done.5, bf16[1024,256]{1,0:T(8,128)(2,1)} %get-tuple-element.18.refs_0_.refs_1_.fine_in, bf16[144,256]{1,0:T(8,128)(2,1)} %get-tuple-element.16.refs_1_.refs_2_.high_in, s32[1168,16]{1,0:T(8,128)} %get-tuple-element.19.refs_2_.refs_4_.pairs_in, ...), custom_call_target="tpu_custom_call" | custom-call | flops 2684354560 | bytes 4194304 | tf_op jit(solution)/shard_map/own_pass/pallas_call | solution.py:217
  41.1 3.3 %all-to-all-done.asked_ref = s32[32,1,16]{2,1,0:T(1,128)S(1)} async-done(((s32[32,1,16]{2,1,0:T(1,128)}), s32[32,1,16]{2,1,0:T(1,128)S(1)}, u32[]{:S(2)}, u32[]{:S(2)}) %all-to-all-start) | async-done | bytes 2080 | tf_op jit(solution)/shard_map/all_to_all | solution.py:406
  44.4 0.0 copy-start.4
  44.4 8.0 %all-to-all-start.3 = ((bf16[12,32,256]{2,1,0:T(8,128)(2,1)}), bf16[12,32,256]{2,1,0:T(8,128)(2,1)S(1)}, u32[]{:S(2)}, u32[]{:S(2)}) async-start(bf16[12,32,256]{2,1,0:T(8,128)(2,1)} %bitcast.9), calls=%async_computation.3 | async-start | bytes 393216 | tf_op jit(solution)/shard_map/all_to_all | solution.py:406
  52.4 0.0 collective-permute-done.refs_3_
  52.4 0.0 copy-start.6
  52.4 0.0 copy-done.4
  52.5 0.6 copy-done.6
  53.1 11.5 %own_pass.3 = (bf16[512,256]{1,0:T(8,128)(2,1)}, f32[1024,256]{1,0:T(8,128)}) custom-call(s32[32,1,16]{2,1,0:T(1,128)} %copy-done.4, s32[1]{0:T(128)} %bitcast.1.refs_0_, bf16[1024,256]{1,0:T(8,128)(2,1)} %get-tuple-element.18.refs_0_.refs_1_.fine_in, bf16[144,256]{1,0:T(8,128)(2,1)} %get-tuple-element.16.refs_1_.refs_2_.high_in, ...), custom_call_target="tpu_custom_call" | custom-call | flops 6710886400 | bytes 4194304 | tf_op jit(solution)/shard_map/own_pass/pallas_call | solution.py:217
  64.6 0.0 copy-start
  64.6 0.0 copy-start.1
  64.6 0.0 copy-start.2
  64.7 0.5 all-to-all-done.3
  65.2 0.0 copy-start.3
  65.2 0.7 copy-done.3
  65.9 7.4 %all-to-all-start.2 = ((bf16[32,16,256]{2,1,0:T(8,128)(2,1)}), bf16[32,16,256]{2,1,0:T(8,128)(2,1)S(1)}, u32[]{:S(2)}, u32[]{:S(2)}) async-start(bf16[32,16,256]{2,1,0:T(8,128)(2,1)} %bitcast.7), calls=%async_computation.2 | async-start | bytes 524288 | tf_op jit(solution)/shard_map/all_to_all | solution.py:406
  73.3 8.7 %near_pass.1.sums_in = f32[8192,256]{1,0:T(8,128)} custom-call(bf16[384,256]{1,0:T(8,128)(2,1)} %bitcast.8, bf16[1024,256]{1,0:T(8,128)(2,1)} %get-tuple-element.18.refs_0_.refs_1_.fine_in, bf16[144,256]{1,0:T(8,128)(2,1)} %get-tuple-element.16.refs_1_.refs_2_.high_in, s32[1168,16]{1,0:T(8,128)} %get-tuple-element.19.refs_2_.refs_4_.pairs_in, ...), custom_call_target="tpu_custom_call" | custom-call | flops 3825205248 | bytes 6291456 | tf_op jit(solution)/shard_map/near_pass/pallas_call | solution.py:312
  82.0 3.9 %all-to-all-done.2 = bf16[32,16,256]{2,1,0:T(8,128)(2,1)S(1)} async-done(((bf16[32,16,256]{2,1,0:T(8,128)(2,1)}), bf16[32,16,256]{2,1,0:T(8,128)(2,1)S(1)}, u32[]{:S(2)}, u32[]{:S(2)}) %all-to-all-start.2) | async-done | bytes 262176 | tf_op jit(solution)/shard_map/all_to_all | solution.py:406
  85.8 0.0 copy-done
  85.8 0.0 copy-done.1
  85.8 0.0 copy-done.2
  85.8 3.1 %far_pass.1 = bf16[1024,256]{1,0:T(8,128)(2,1)} custom-call(s32[1]{0:T(128)S(6)} %copy.9.live_ref, bf16[512,256]{1,0:T(8,128)(2,1)S(1)} %bitcast.6, s32[144,16]{1,0:T(8,128)S(1)} %copy-done.2, bf16[16,256,256]{2,1,0:T(8,128)(2,1)S(1)} %copy-done, bf16[8,256,256]{2,1,0:T(8,128)(2,1)S(1)} %copy-done.1, f32[8192,256]{1,0:T(8,128)} %near_pass.1.sums_in), custom_call_target="tpu_custom_call" | custom-call | flops 1040187392 | bytes 6291456 | tf_op jit(solution)/shard_map/far_pass/pallas_call | solution.py:384
Async XLA Ops:
  1.3 23.4 %all-to-all-start.1 = ((s32[12,1,32]{2,1,0:T(1,128)}), s32[12,1,32]{2,1,0:T(1,128)S(1)}, u32[]{:S(2)}, u32[]{:S(2)}) async-start(s32[12,1,32]{2,1,0:T(1,128)} %broadcast_in_dim.3), calls=%async_computation.1 | async-start | bytes 12288 | tf_op jit(solution)/shard_map/all_to_all | solution.py:406
  21.1 31.3 %collective-permute-start = (bf16[144,256]{1,0:T(8,128)(2,1)}, bf16[144,256]{1,0:T(8,128)(2,1)S(1)}, u32[]{:S(2)}, u32[]{:S(2)}) collective-permute-start(bf16[144,256]{1,0:T(8,128)(2,1)} %get-tuple-element.16.refs_1_.refs_2_.high_in), channel_id=1, source_target_pairs={{0,12},{12,0},{1,13},{13,1},{2,14},{14,2},{3,15},{15,3},{4,16},{16... | collective-permute-start | bytes 221192 | tf_op jit(solution)/shard_map/ppermute | solution.py:426
  24.7 10.0 %copy-start.5 = (s32[12,1,32]{2,1,0:T(1,128)}, s32[12,1,32]{2,1,0:T(1,128)S(1)}, u32[]{:S(2)}) copy-start(s32[12,1,32]{2,1,0:T(1,128)S(1)} %all-to-all-done.1.asked_ref) | copy-start | bytes 4612
  24.7 19.7 %all-to-all-start = ((s32[32,1,16]{2,1,0:T(1,128)}), s32[32,1,16]{2,1,0:T(1,128)S(1)}, u32[]{:S(2)}, u32[]{:S(2)}) async-start(s32[32,1,16]{2,1,0:T(1,128)} %get-tuple-element.17), calls=%async_computation | async-start | bytes 32768 | tf_op jit(solution)/shard_map/all_to_all | solution.py:406
  44.4 8.0 %copy-start.4 = (s32[32,1,16]{2,1,0:T(1,128)}, s32[32,1,16]{2,1,0:T(1,128)S(1)}, u32[]{:S(2)}) copy-start(s32[32,1,16]{2,1,0:T(1,128)S(1)} %all-to-all-done.asked_ref) | copy-start | bytes 6148
  44.4 20.8 %all-to-all-start.3 = ((bf16[12,32,256]{2,1,0:T(8,128)(2,1)}), bf16[12,32,256]{2,1,0:T(8,128)(2,1)S(1)}, u32[]{:S(2)}, u32[]{:S(2)}) async-start(bf16[12,32,256]{2,1,0:T(8,128)(2,1)} %bitcast.9), calls=%async_computation.3 | async-start | bytes 393216 | tf_op jit(solution)/shard_map/all_to_all | solution.py:406
  52.4 0.6 copy-start.6
  64.6 21.2 %copy-start = (bf16[16,256,256]{2,1,0:T(8,128)(2,1)S(1)}, bf16[16,256,256]{2,1,0:T(8,128)(2,1)}, u32[]{:S(2)}) copy-start(bf16[16,256,256]{2,1,0:T(8,128)(2,1)} %ops.1) | copy-start | bytes 6291460
  64.6 21.2 %copy-start.1 = (bf16[8,256,256]{2,1,0:T(8,128)(2,1)S(1)}, bf16[8,256,256]{2,1,0:T(8,128)(2,1)}, u32[]{:S(2)}) copy-start(bf16[8,256,256]{2,1,0:T(8,128)(2,1)} %down.1) | copy-start | bytes 3145732
  64.6 21.2 %copy-start.2 = (s32[144,16]{1,0:T(8,128)S(1)}, s32[144,16]{1,0:T(8,128)}, u32[]{:S(2)}) copy-start(s32[144,16]{1,0:T(8,128)} %get-tuple-element.22.pairs) | copy-start | bytes 27652
  65.2 0.7 copy-start.3
  65.9 20.0 %all-to-all-start.2 = ((bf16[32,16,256]{2,1,0:T(8,128)(2,1)}), bf16[32,16,256]{2,1,0:T(8,128)(2,1)S(1)}, u32[]{:S(2)}, u32[]{:S(2)}) async-start(bf16[32,16,256]{2,1,0:T(8,128)(2,1)} %bitcast.7), calls=%async_computation.2 | async-start | bytes 524288 | tf_op jit(solution)/shard_map/all_to_all | solution.py:406

commit v5 on v4

--- a/solution.py
+++ b/solution.py
@@ -17,7 +17,7 @@
 ANY = pl.BlockSpec(memory_space=pl.ANY)
 VMEM = pl.BlockSpec(memory_space=pltpu.VMEM)
 SMEM = pl.BlockSpec(memory_space=pltpu.SMEM)
-TIGHT = pltpu.CompilerParams(vmem_limit_bytes=51000 << 10)
+TIGHT = pltpu.CompilerParams(vmem_limit_bytes=52500 << 10)
 PARAMS = pltpu.CompilerParams(vmem_limit_bytes=56 << 20)
 
 
@@ -332,21 +332,26 @@
     )(near, fine, high, pairs, ops, total)
 
 
-def far_kernel(base, live_ref, far_ref, pairs, ops, down, sums_in, out_out,
-               mid, total, out, picked, mid_wide, fine_wide, sems, out_sems):
+def far_kernel(base, live_ref, far_ref, pairs, down, ops_in, sums_in, out_out,
+               ops, mid, total, out, picked, mid_wide, fine_wide, sems, op_sems, out_sems):
     count = total.shape[0]
     middles = mid.shape[0]
     cells = pairs.shape[0]
     offsets = ops.shape[0]
+    get_ops = [start(ops_in.at[o], ops.at[o], op_sems.at[o]) for o in range(offsets)]
     get_mid = start(sums_in.at[pl.ds(count, middles)], mid, sems.at[0])
     get_total = start(sums_in.at[pl.ds(0, count)], total, sems.at[1])
     place = pairs[...] - base
     for o in range(offsets):
         hot = one_hot([place[:, o : o + 1]], 0, far_ref.shape[0])
         picked[o] = dot(hot, far_ref[...]).astype(BF16)
-    field = dot(picked[0], ops[0])
-    for o in range(1, offsets):
-        field = field + dot(picked[o], ops[o])
+    field = None
+    for o in range(offsets):
+        if o % 4 == 0:
+            for get in get_ops[o : o + 4]:
+                get.wait()
+        term = dot(picked[o], ops[o])
+        field = term if field is None else field + term
     get_mid.wait()
     coarse = field[middles:, :].astype(BF16)
     for k in range(8):
@@ -384,9 +389,10 @@
     return pl.pallas_call(
         functools.partial(far_kernel, base),
         out_shape=jax.ShapeDtypeStruct((count, size), BF16),
-        in_specs=[SMEM] + [VMEM] * 4 + [ANY],
+        in_specs=[SMEM] + [VMEM] * 3 + [ANY] * 2,
         out_specs=ANY,
         scratch_shapes=[
+            pltpu.VMEM(ops.shape, BF16),
             pltpu.VMEM((middles, size), F32),
             pltpu.VMEM((count, size), F32),
             pltpu.VMEM((count, size), BF16),
@@ -394,12 +400,13 @@
             pltpu.VMEM((2, middles, 128), F32),
             pltpu.VMEM((2, count, 128), F32),
             pltpu.SemaphoreType.DMA((2,)),
+            pltpu.SemaphoreType.DMA((offsets,)),
             pltpu.SemaphoreType.DMA((count // TILE,)),
         ],
         compiler_params=TIGHT,
         cost_estimate=cost(macs, 6 << 20),
         name="far_pass",
-    )(live, far, pairs, ops, down, sums)
+    )(live, far, pairs, down, ops, sums)
 
 
 def exchange(rows, axis):

time: 89.7 us -> 90.4 us (level)
  Pallas kernels: 34.1 us -> 35.5 us
    pallas_call x1, Pallas kernels: 3.08 us -> 4.41 us  [far_pass(): pl.pallas_call(functools.partial(far_kernel, base), out_shape=jax.ShapeDt...]
where the time goes in v5:
time: 90.4 us; the launch traced here: 89.7 us
  starting transfers between devices  42.1 us (47%)
  Pallas kernels  35.5 us (39%)
  waiting for transfers between devices  9.34 us (10%)
  local copies, waits for them, and re-layouts  1.93 us (2%)
  between operations  0.93 us (1%)
    all_to_all x4, starting transfers between devices, exchange(): return lax.all_to_all(rows, axis, split_axis=0, concat_axis=0, tiled=True)  40.1 us
    pallas_call x2, Pallas kernels, own_pass(): pl.pallas_call(functools.partial(own_kernel, first, offsets), out_shape=(...  18 us
    all_to_all x4, waiting for transfers between devices, exchange(): return lax.all_to_all(rows, axis, split_axis=0, concat_axis=0, tiled=True)  9.34 us
    pallas_call x1, Pallas kernels, near_pass(): pl.pallas_call(functools.partial(near_kernel, base, asked, own), out_shap...  8.66 us
    pallas_call x1, Pallas kernels, up_pass(): pl.pallas_call(up_kernel, out_shape=(jax.ShapeDtypeStruct((count, size),...  4.42 us
    pallas_call x1, Pallas kernels, far_pass(): pl.pallas_call(functools.partial(far_kernel, base), out_shape=jax.ShapeDt...  4.41 us
    ppermute x1, starting transfers between devices, body(): other = lax.ppermute(high, 'core', [(0, 1), (1, 0)])  1.92 us
  transfers between devices with their start and end apart: 5, of which 4 were waited for; matrix products, arithmetic and copies ran while one was open for 0% of the time, Pallas kernels for 35%

profile of v5, /device:TPU:64, one launch (start us, length us, event | category | flops | bytes accessed | tf_op | source)
XLA Modules:
  0.0 89.7 jit_solution(16844492967739234970)
XLA Ops:
  0.0 1.3 %broadcast_in_dim.3 = s32[12,1,32]{2,1,0:T(1,128)} reshape(s32[12,32]{1,0:T(8,128)} %param.10) | data formatting | bytes 3072 | tf_op jit(solution)/shard_map/broadcast_in_dim | solution.py:429
  1.3 14.8 %all-to-all-start.1 = ((s32[12,1,32]{2,1,0:T(1,128)}), s32[12,1,32]{2,1,0:T(1,128)S(1)}, u32[]{:S(2)}, u32[]{:S(2)}) async-start(s32[12,1,32]{2,1,0:T(1,128)} %broadcast_in_dim.3), calls=%async_computation.1 | async-start | bytes 12288 | tf_op jit(solution)/shard_map/all_to_all | solution.py:413
  16.7 4.4 %up_pass.1 = (bf16[1024,256]{1,0:T(8,128)(2,1)}, bf16[144,256]{1,0:T(8,128)(2,1)}, s32[1168,16]{1,0:T(8,128)}, s32[144,16]{1,0:T(8,128)}, s32[32,1,16]{2,1,0:T(1,128)}) custom-call(s32[1]{0:T(128)S(6)} %copy.9.live_ref, s32[16,1168]{1,0:T(8,128)} %source_ref.1, s32[8,64]{1,0:T(8,128)} %bitcast.10, bf16[1024,256]{1,0:T(8,128)(2,1)} %moments_in.1, ...), custom_call_target="tpu_custom_call" | custom-call | flops 134217728 | bytes 3145728 | tf_op jit(solution)/shard_map/up_pass/pallas_call | solution.py:114
  21.1 1.9 %collective-permute-start = (bf16[144,256]{1,0:T(8,128)(2,1)}, bf16[144,256]{1,0:T(8,128)(2,1)S(1)}, u32[]{:S(2)}, u32[]{:S(2)}) collective-permute-start(bf16[144,256]{1,0:T(8,128)(2,1)} %get-tuple-element.16.refs_1_.refs_2_.high_in), channel_id=1, source_target_pairs={{0,12},{12,0},{1,13},{13,1},{2,14},{14,2},{3,15},{15,3},{4,16},{16... | collective-permute-start | bytes 221192 | tf_op jit(solution)/shard_map/ppermute | solution.py:433
  23.1 1.6 %all-to-all-done.1.asked_ref = s32[12,1,32]{2,1,0:T(1,128)S(1)} async-done(((s32[12,1,32]{2,1,0:T(1,128)}), s32[12,1,32]{2,1,0:T(1,128)S(1)}, u32[]{:S(2)}, u32[]{:S(2)}) %all-to-all-start.1) | async-done | bytes 1568 | tf_op jit(solution)/shard_map/all_to_all | solution.py:413
  24.7 0.0 copy-start.4
  24.7 10.0 %all-to-all-start = ((s32[32,1,16]{2,1,0:T(1,128)}), s32[32,1,16]{2,1,0:T(1,128)S(1)}, u32[]{:S(2)}, u32[]{:S(2)}) async-start(s32[32,1,16]{2,1,0:T(1,128)} %get-tuple-element.17), calls=%async_computation | async-start | bytes 32768 | tf_op jit(solution)/shard_map/all_to_all | solution.py:413
  34.7 0.0 copy-done.4
  34.7 6.4 %own_pass.2 = (bf16[384,256]{1,0:T(8,128)(2,1)}, f32[1024,256]{1,0:T(8,128)}) custom-call(s32[12,1,32]{2,1,0:T(1,128)} %copy-done.4, bf16[1024,256]{1,0:T(8,128)(2,1)} %get-tuple-element.18.refs_0_.refs_1_.fine_in, bf16[144,256]{1,0:T(8,128)(2,1)} %get-tuple-element.16.refs_1_.refs_2_.high_in, s32[1168,16]{1,0:T(8,128)} %get-tuple-element.19.refs_2_.refs_4_.pairs_in, ...), custom_call_target="tpu_custom_call" | custom-call | flops 2684354560 | bytes 4194304 | tf_op jit(solution)/shard_map/own_pass/pallas_call | solution.py:217
  41.1 3.3 %all-to-all-done.asked_ref = s32[32,1,16]{2,1,0:T(1,128)S(1)} async-done(((s32[32,1,16]{2,1,0:T(1,128)}), s32[32,1,16]{2,1,0:T(1,128)S(1)}, u32[]{:S(2)}, u32[]{:S(2)}) %all-to-all-start) | async-done | bytes 2080 | tf_op jit(solution)/shard_map/all_to_all | solution.py:413
  44.4 0.0 copy-start.3
  44.4 8.0 %all-to-all-start.3 = ((bf16[12,32,256]{2,1,0:T(8,128)(2,1)}), bf16[12,32,256]{2,1,0:T(8,128)(2,1)S(1)}, u32[]{:S(2)}, u32[]{:S(2)}) async-start(bf16[12,32,256]{2,1,0:T(8,128)(2,1)} %bitcast.9), calls=%async_computation.3 | async-start | bytes 393216 | tf_op jit(solution)/shard_map/all_to_all | solution.py:413
  52.4 0.0 collective-permute-done.refs_3_
  52.4 0.0 copy-start.5
  52.5 0.0 copy-done.3
  52.5 0.6 copy-done.5
  53.1 11.5 %own_pass.3 = (bf16[512,256]{1,0:T(8,128)(2,1)}, f32[1024,256]{1,0:T(8,128)}) custom-call(s32[32,1,16]{2,1,0:T(1,128)} %copy-done.3, s32[1]{0:T(128)} %bitcast.1.refs_0_, bf16[1024,256]{1,0:T(8,128)(2,1)} %get-tuple-element.18.refs_0_.refs_1_.fine_in, bf16[144,256]{1,0:T(8,128)(2,1)} %get-tuple-element.16.refs_1_.refs_2_.high_in, ...), custom_call_target="tpu_custom_call" | custom-call | flops 6710886400 | bytes 4194304 | tf_op jit(solution)/shard_map/own_pass/pallas_call | solution.py:217
  64.6 0.0 copy-start
  64.6 0.0 copy-start.1
  64.7 0.5 all-to-all-done.3
  65.2 0.0 copy-start.2
  65.2 7.4 %all-to-all-start.2 = ((bf16[32,16,256]{2,1,0:T(8,128)(2,1)}), bf16[32,16,256]{2,1,0:T(8,128)(2,1)S(1)}, u32[]{:S(2)}, u32[]{:S(2)}) async-start(bf16[32,16,256]{2,1,0:T(8,128)(2,1)} %bitcast.7), calls=%async_computation.2 | async-start | bytes 524288 | tf_op jit(solution)/shard_map/all_to_all | solution.py:413
  72.6 0.0 copy-done.2
  72.6 8.7 %near_pass.1.sums_in = f32[8192,256]{1,0:T(8,128)} custom-call(bf16[384,256]{1,0:T(8,128)(2,1)} %bitcast.8, bf16[1024,256]{1,0:T(8,128)(2,1)} %get-tuple-element.18.refs_0_.refs_1_.fine_in, bf16[144,256]{1,0:T(8,128)(2,1)} %get-tuple-element.16.refs_1_.refs_2_.high_in, s32[1168,16]{1,0:T(8,128)} %get-tuple-element.19.refs_2_.refs_4_.pairs_in, ...), custom_call_target="tpu_custom_call" | custom-call | flops 3825205248 | bytes 6291456 | tf_op jit(solution)/shard_map/near_pass/pallas_call | solution.py:312
  81.3 3.9 %all-to-all-done.2 = bf16[32,16,256]{2,1,0:T(8,128)(2,1)S(1)} async-done(((bf16[32,16,256]{2,1,0:T(8,128)(2,1)}), bf16[32,16,256]{2,1,0:T(8,128)(2,1)S(1)}, u32[]{:S(2)}, u32[]{:S(2)}) %all-to-all-start.2) | async-done | bytes 262176 | tf_op jit(solution)/shard_map/all_to_all | solution.py:413
  85.2 0.0 copy-done
  85.2 0.0 copy-done.1
  85.2 4.4 %far_pass.1 = bf16[1024,256]{1,0:T(8,128)(2,1)} custom-call(s32[1]{0:T(128)S(6)} %copy.9.live_ref, bf16[512,256]{1,0:T(8,128)(2,1)S(1)} %bitcast.6, s32[144,16]{1,0:T(8,128)S(1)} %copy-done.1, bf16[8,256,256]{2,1,0:T(8,128)(2,1)S(1)} %copy-done, bf16[16,256,256]{2,1,0:T(8,128)(2,1)} %ops_in.3, f32[8192,256]{1,0:T(8,128)} %near_pass.1.sums_in), custom_call_target="tpu_custom_call" | custom-call | flops 1040187392 | bytes 6291456 | tf_op jit(solution)/shard_map/far_pass/pallas_call | solution.py:389
Async XLA Ops:
  1.3 23.4 %all-to-all-start.1 = ((s32[12,1,32]{2,1,0:T(1,128)}), s32[12,1,32]{2,1,0:T(1,128)S(1)}, u32[]{:S(2)}, u32[]{:S(2)}) async-start(s32[12,1,32]{2,1,0:T(1,128)} %broadcast_in_dim.3), calls=%async_computation.1 | async-start | bytes 12288 | tf_op jit(solution)/shard_map/all_to_all | solution.py:413
  21.1 31.3 %collective-permute-start = (bf16[144,256]{1,0:T(8,128)(2,1)}, bf16[144,256]{1,0:T(8,128)(2,1)S(1)}, u32[]{:S(2)}, u32[]{:S(2)}) collective-permute-start(bf16[144,256]{1,0:T(8,128)(2,1)} %get-tuple-element.16.refs_1_.refs_2_.high_in), channel_id=1, source_target_pairs={{0,12},{12,0},{1,13},{13,1},{2,14},{14,2},{3,15},{15,3},{4,16},{16... | collective-permute-start | bytes 221192 | tf_op jit(solution)/shard_map/ppermute | solution.py:433
  24.7 10.0 %copy-start.4 = (s32[12,1,32]{2,1,0:T(1,128)}, s32[12,1,32]{2,1,0:T(1,128)S(1)}, u32[]{:S(2)}) copy-start(s32[12,1,32]{2,1,0:T(1,128)S(1)} %all-to-all-done.1.asked_ref) | copy-start | bytes 4612
  24.7 19.7 %all-to-all-start = ((s32[32,1,16]{2,1,0:T(1,128)}), s32[32,1,16]{2,1,0:T(1,128)S(1)}, u32[]{:S(2)}, u32[]{:S(2)}) async-start(s32[32,1,16]{2,1,0:T(1,128)} %get-tuple-element.17), calls=%async_computation | async-start | bytes 32768 | tf_op jit(solution)/shard_map/all_to_all | solution.py:413
  44.4 8.0 %copy-start.3 = (s32[32,1,16]{2,1,0:T(1,128)}, s32[32,1,16]{2,1,0:T(1,128)S(1)}, u32[]{:S(2)}) copy-start(s32[32,1,16]{2,1,0:T(1,128)S(1)} %all-to-all-done.asked_ref) | copy-start | bytes 6148
  44.4 20.7 %all-to-all-start.3 = ((bf16[12,32,256]{2,1,0:T(8,128)(2,1)}), bf16[12,32,256]{2,1,0:T(8,128)(2,1)S(1)}, u32[]{:S(2)}, u32[]{:S(2)}) async-start(bf16[12,32,256]{2,1,0:T(8,128)(2,1)} %bitcast.9), calls=%async_computation.3 | async-start | bytes 393216 | tf_op jit(solution)/shard_map/all_to_all | solution.py:413
  52.4 0.6 copy-start.5
  64.6 20.5 %copy-start = (bf16[8,256,256]{2,1,0:T(8,128)(2,1)S(1)}, bf16[8,256,256]{2,1,0:T(8,128)(2,1)}, u32[]{:S(2)}) copy-start(bf16[8,256,256]{2,1,0:T(8,128)(2,1)} %down.1) | copy-start | bytes 3145732
  64.6 20.5 %copy-start.1 = (s32[144,16]{1,0:T(8,128)S(1)}, s32[144,16]{1,0:T(8,128)}, u32[]{:S(2)}) copy-start(s32[144,16]{1,0:T(8,128)} %get-tuple-element.22.pairs) | copy-start | bytes 27652
  65.2 7.4 %copy-start.2 = (bf16[12,32,256]{2,1,0:T(8,128)(2,1)}, bf16[12,32,256]{2,1,0:T(8,128)(2,1)S(1)}, u32[]{:S(2)}) copy-start(bf16[12,32,256]{2,1,0:T(8,128)(2,1)S(1)} %all-to-all-done.3) | copy-start | bytes 589828
  65.2 20.0 %all-to-all-start.2 = ((bf16[32,16,256]{2,1,0:T(8,128)(2,1)}), bf16[32,16,256]{2,1,0:T(8,128)(2,1)S(1)}, u32[]{:S(2)}, u32[]{:S(2)}) async-start(bf16[32,16,256]{2,1,0:T(8,128)(2,1)} %bitcast.7), calls=%async_computation.2 | async-start | bytes 524288 | tf_op jit(solution)/shard_map/all_to_all | solution.py:413

commit v6 on v4

--- a/solution.py
+++ b/solution.py
@@ -12,8 +12,8 @@
 F32 = jnp.float32
 I32 = jnp.int32
 TILE = 256
-EARLY = 4
-LAST = 14
+EARLY = 5
+LAST = 15
 ANY = pl.BlockSpec(memory_space=pl.ANY)
 VMEM = pl.BlockSpec(memory_space=pltpu.VMEM)
 SMEM = pl.BlockSpec(memory_space=pltpu.SMEM)

time: 89.7 us -> 90.6 us (1.010)
  starting transfers between devices: 42.1 us -> 43.1 us
    all_to_all x4, starting transfers between devices: 40.2 us -> 41.2 us  [exchange(): return lax.all_to_all(rows, axis, split_axis=0, concat_axis=0, tiled=True)]
  transfers between devices with their start and end apart: 5 -> 5, of which waited for: 4 -> 4; matrix products, arithmetic and copies ran while one was open for 0% -> 0% of each run, Pallas kernels for 35% -> 34%
where the time goes in v6:
time: 90.6 us; the launch traced here: 89.9 us
  starting transfers between devices  43.1 us (48%)
  Pallas kernels  34.1 us (38%)
  waiting for transfers between devices  9.16 us (10%)
  local copies, waits for them, and re-layouts  2.62 us (3%)
  between operations  0.96 us (1%)
    all_to_all x4, starting transfers between devices, exchange(): return lax.all_to_all(rows, axis, split_axis=0, concat_axis=0, tiled=True)  41.2 us
    pallas_call x2, Pallas kernels, own_pass(): pl.pallas_call(functools.partial(own_kernel, first, offsets), out_shape=(...  18.8 us
    all_to_all x4, waiting for transfers between devices, exchange(): return lax.all_to_all(rows, axis, split_axis=0, concat_axis=0, tiled=True)  9.15 us
    pallas_call x1, Pallas kernels, near_pass(): pl.pallas_call(functools.partial(near_kernel, base, asked, own), out_shap...  7.8 us
    pallas_call x1, Pallas kernels, up_pass(): pl.pallas_call(up_kernel, out_shape=(jax.ShapeDtypeStruct((count, size),...  4.41 us
    pallas_call x1, Pallas kernels, far_pass(): pl.pallas_call(functools.partial(far_kernel, base), out_shape=jax.ShapeDt...  3.08 us
    ppermute x1, starting transfers between devices, body(): other = lax.ppermute(high, 'core', [(0, 1), (1, 0)])  1.92 us
  transfers between devices with their start and end apart: 5, of which 4 were waited for; matrix products, arithmetic and copies ran while one was open for 0% of the time, Pallas kernels for 34%

profile of v6, /device:TPU:64, one launch (start us, length us, event | category | flops | bytes accessed | tf_op | source)
XLA Modules:
  0.0 89.9 jit_solution(10017456832879571600)
XLA Ops:
  0.0 1.3 %broadcast_in_dim.3 = s32[12,1,32]{2,1,0:T(1,128)} reshape(s32[12,32]{1,0:T(8,128)} %param.10) | data formatting | bytes 3072 | tf_op jit(solution)/shard_map/broadcast_in_dim | solution.py:422
  1.3 14.8 %all-to-all-start.1 = ((s32[12,1,32]{2,1,0:T(1,128)}), s32[12,1,32]{2,1,0:T(1,128)S(1)}, u32[]{:S(2)}, u32[]{:S(2)}) async-start(s32[12,1,32]{2,1,0:T(1,128)} %broadcast_in_dim.3), calls=%async_computation.1 | async-start | bytes 12288 | tf_op jit(solution)/shard_map/all_to_all | solution.py:406
  16.7 4.4 %up_pass.1 = (bf16[1024,256]{1,0:T(8,128)(2,1)}, bf16[144,256]{1,0:T(8,128)(2,1)}, s32[1168,16]{1,0:T(8,128)}, s32[144,16]{1,0:T(8,128)}, s32[32,1,16]{2,1,0:T(1,128)}) custom-call(s32[1]{0:T(128)S(6)} %copy.9.live_ref, s32[16,1168]{1,0:T(8,128)} %source_ref.1, s32[8,64]{1,0:T(8,128)} %bitcast.10, bf16[1024,256]{1,0:T(8,128)(2,1)} %moments_in.1, ...), custom_call_target="tpu_custom_call" | custom-call | flops 134217728 | bytes 3145728 | tf_op jit(solution)/shard_map/up_pass/pallas_call | solution.py:114
  21.1 1.9 %collective-permute-start = (bf16[144,256]{1,0:T(8,128)(2,1)}, bf16[144,256]{1,0:T(8,128)(2,1)S(1)}, u32[]{:S(2)}, u32[]{:S(2)}) collective-permute-start(bf16[144,256]{1,0:T(8,128)(2,1)} %get-tuple-element.16.refs_1_.refs_2_.high_in), channel_id=1, source_target_pairs={{0,12},{12,0},{1,13},{13,1},{2,14},{14,2},{3,15},{15,3},{4,16},{16... | collective-permute-start | bytes 221192 | tf_op jit(solution)/shard_map/ppermute | solution.py:426
  23.1 1.6 %all-to-all-done.1.asked_ref = s32[12,1,32]{2,1,0:T(1,128)S(1)} async-done(((s32[12,1,32]{2,1,0:T(1,128)}), s32[12,1,32]{2,1,0:T(1,128)S(1)}, u32[]{:S(2)}, u32[]{:S(2)}) %all-to-all-start.1) | async-done | bytes 1568 | tf_op jit(solution)/shard_map/all_to_all | solution.py:406
  24.7 0.0 copy-start.5
  24.7 10.0 %all-to-all-start = ((s32[32,1,16]{2,1,0:T(1,128)}), s32[32,1,16]{2,1,0:T(1,128)S(1)}, u32[]{:S(2)}, u32[]{:S(2)}) async-start(s32[32,1,16]{2,1,0:T(1,128)} %get-tuple-element.17), calls=%async_computation | async-start | bytes 32768 | tf_op jit(solution)/shard_map/all_to_all | solution.py:406
  34.7 0.0 copy-done.5
  34.7 7.2 %own_pass.2 = (bf16[384,256]{1,0:T(8,128)(2,1)}, f32[1024,256]{1,0:T(8,128)}) custom-call(s32[12,1,32]{2,1,0:T(1,128)} %copy-done.5, bf16[1024,256]{1,0:T(8,128)(2,1)} %get-tuple-element.18.refs_0_.refs_1_.fine_in, bf16[144,256]{1,0:T(8,128)(2,1)} %get-tuple-element.16.refs_1_.refs_2_.high_in, s32[1168,16]{1,0:T(8,128)} %get-tuple-element.19.refs_2_.refs_4_.pairs_in, ...), custom_call_target="tpu_custom_call" | custom-call | flops 3355443200 | bytes 4194304 | tf_op jit(solution)/shard_map/own_pass/pallas_call | solution.py:217
  41.9 2.5 %all-to-all-done.asked_ref = s32[32,1,16]{2,1,0:T(1,128)S(1)} async-done(((s32[32,1,16]{2,1,0:T(1,128)}), s32[32,1,16]{2,1,0:T(1,128)S(1)}, u32[]{:S(2)}, u32[]{:S(2)}) %all-to-all-start) | async-done | bytes 2080 | tf_op jit(solution)/shard_map/all_to_all | solution.py:406
  44.4 0.0 copy-start.4
  44.4 8.0 %all-to-all-start.3 = ((bf16[12,32,256]{2,1,0:T(8,128)(2,1)}), bf16[12,32,256]{2,1,0:T(8,128)(2,1)S(1)}, u32[]{:S(2)}, u32[]{:S(2)}) async-start(bf16[12,32,256]{2,1,0:T(8,128)(2,1)} %bitcast.9), calls=%async_computation.3 | async-start | bytes 393216 | tf_op jit(solution)/shard_map/all_to_all | solution.py:406
  52.4 0.0 collective-permute-done.refs_3_
  52.4 0.0 copy-start.6
  52.4 0.0 copy-done.4
  52.5 0.6 copy-done.6
  53.1 11.5 %own_pass.3 = (bf16[512,256]{1,0:T(8,128)(2,1)}, f32[1024,256]{1,0:T(8,128)}) custom-call(s32[32,1,16]{2,1,0:T(1,128)} %copy-done.4, s32[1]{0:T(128)} %bitcast.1.refs_0_, bf16[1024,256]{1,0:T(8,128)(2,1)} %get-tuple-element.18.refs_0_.refs_1_.fine_in, bf16[144,256]{1,0:T(8,128)(2,1)} %get-tuple-element.16.refs_1_.refs_2_.high_in, ...), custom_call_target="tpu_custom_call" | custom-call | flops 6710886400 | bytes 4194304 | tf_op jit(solution)/shard_map/own_pass/pallas_call | solution.py:217
  64.6 0.0 copy-start
  64.6 0.0 copy-start.1
  64.6 0.0 copy-start.2
  64.7 0.5 all-to-all-done.3
  65.2 0.0 copy-start.3
  65.2 0.7 copy-done.3
  65.9 8.4 %all-to-all-start.2 = ((bf16[32,16,256]{2,1,0:T(8,128)(2,1)}), bf16[32,16,256]{2,1,0:T(8,128)(2,1)S(1)}, u32[]{:S(2)}, u32[]{:S(2)}) async-start(bf16[32,16,256]{2,1,0:T(8,128)(2,1)} %bitcast.7), calls=%async_computation.2 | async-start | bytes 524288 | tf_op jit(solution)/shard_map/all_to_all | solution.py:406
  74.3 7.8 %near_pass.1.sums_in = f32[8192,256]{1,0:T(8,128)} custom-call(bf16[384,256]{1,0:T(8,128)(2,1)} %bitcast.8, bf16[1024,256]{1,0:T(8,128)(2,1)} %get-tuple-element.18.refs_0_.refs_1_.fine_in, bf16[144,256]{1,0:T(8,128)(2,1)} %get-tuple-element.16.refs_1_.refs_2_.high_in, s32[1168,16]{1,0:T(8,128)} %get-tuple-element.19.refs_2_.refs_4_.pairs_in, ...), custom_call_target="tpu_custom_call" | custom-call | flops 3825205248 | bytes 6291456 | tf_op jit(solution)/shard_map/near_pass/pallas_call | solution.py:312
  82.1 4.5 %all-to-all-done.2 = bf16[32,16,256]{2,1,0:T(8,128)(2,1)S(1)} async-done(((bf16[32,16,256]{2,1,0:T(8,128)(2,1)}), bf16[32,16,256]{2,1,0:T(8,128)(2,1)S(1)}, u32[]{:S(2)}, u32[]{:S(2)}) %all-to-all-start.2) | async-done | bytes 262176 | tf_op jit(solution)/shard_map/all_to_all | solution.py:406
  86.6 0.0 copy-done
  86.6 0.0 copy-done.1
  86.6 0.0 copy-done.2
  86.6 3.1 %far_pass.1 = bf16[1024,256]{1,0:T(8,128)(2,1)} custom-call(s32[1]{0:T(128)S(6)} %copy.9.live_ref, bf16[512,256]{1,0:T(8,128)(2,1)S(1)} %bitcast.6, s32[144,16]{1,0:T(8,128)S(1)} %copy-done.2, bf16[16,256,256]{2,1,0:T(8,128)(2,1)S(1)} %copy-done, bf16[8,256,256]{2,1,0:T(8,128)(2,1)S(1)} %copy-done.1, f32[8192,256]{1,0:T(8,128)} %near_pass.1.sums_in), custom_call_target="tpu_custom_call" | custom-call | flops 1040187392 | bytes 6291456 | tf_op jit(solution)/shard_map/far_pass/pallas_call | solution.py:384
Async XLA Ops:
  1.3 23.4 %all-to-all-start.1 = ((s32[12,1,32]{2,1,0:T(1,128)}), s32[12,1,32]{2,1,0:T(1,128)S(1)}, u32[]{:S(2)}, u32[]{:S(2)}) async-start(s32[12,1,32]{2,1,0:T(1,128)} %broadcast_in_dim.3), calls=%async_computation.1 | async-start | bytes 12288 | tf_op jit(solution)/shard_map/all_to_all | solution.py:406
  21.1 31.3 %collective-permute-start = (bf16[144,256]{1,0:T(8,128)(2,1)}, bf16[144,256]{1,0:T(8,128)(2,1)S(1)}, u32[]{:S(2)}, u32[]{:S(2)}) collective-permute-start(bf16[144,256]{1,0:T(8,128)(2,1)} %get-tuple-element.16.refs_1_.refs_2_.high_in), channel_id=1, source_target_pairs={{0,12},{12,0},{1,13},{13,1},{2,14},{14,2},{3,15},{15,3},{4,16},{16... | collective-permute-start | bytes 221192 | tf_op jit(solution)/shard_map/ppermute | solution.py:426
  24.7 10.0 %copy-start.5 = (s32[12,1,32]{2,1,0:T(1,128)}, s32[12,1,32]{2,1,0:T(1,128)S(1)}, u32[]{:S(2)}) copy-start(s32[12,1,32]{2,1,0:T(1,128)S(1)} %all-to-all-done.1.asked_ref) | copy-start | bytes 4612
  24.7 19.7 %all-to-all-start = ((s32[32,1,16]{2,1,0:T(1,128)}), s32[32,1,16]{2,1,0:T(1,128)S(1)}, u32[]{:S(2)}, u32[]{:S(2)}) async-start(s32[32,1,16]{2,1,0:T(1,128)} %get-tuple-element.17), calls=%async_computation | async-start | bytes 32768 | tf_op jit(solution)/shard_map/all_to_all | solution.py:406
  44.4 8.0 %copy-start.4 = (s32[32,1,16]{2,1,0:T(1,128)}, s32[32,1,16]{2,1,0:T(1,128)S(1)}, u32[]{:S(2)}) copy-start(s32[32,1,16]{2,1,0:T(1,128)S(1)} %all-to-all-done.asked_ref) | copy-start | bytes 6148
  44.4 20.8 %all-to-all-start.3 = ((bf16[12,32,256]{2,1,0:T(8,128)(2,1)}), bf16[12,32,256]{2,1,0:T(8,128)(2,1)S(1)}, u32[]{:S(2)}, u32[]{:S(2)}) async-start(bf16[12,32,256]{2,1,0:T(8,128)(2,1)} %bitcast.9), calls=%async_computation.3 | async-start | bytes 393216 | tf_op jit(solution)/shard_map/all_to_all | solution.py:406
  52.4 0.6 copy-start.6
  64.6 22.0 %copy-start = (bf16[16,256,256]{2,1,0:T(8,128)(2,1)S(1)}, bf16[16,256,256]{2,1,0:T(8,128)(2,1)}, u32[]{:S(2)}) copy-start(bf16[16,256,256]{2,1,0:T(8,128)(2,1)} %ops.1) | copy-start | bytes 6291460
  64.6 22.0 %copy-start.1 = (bf16[8,256,256]{2,1,0:T(8,128)(2,1)S(1)}, bf16[8,256,256]{2,1,0:T(8,128)(2,1)}, u32[]{:S(2)}) copy-start(bf16[8,256,256]{2,1,0:T(8,128)(2,1)} %down.1) | copy-start | bytes 3145732
  64.6 22.0 %copy-start.2 = (s32[144,16]{1,0:T(8,128)S(1)}, s32[144,16]{1,0:T(8,128)}, u32[]{:S(2)}) copy-start(s32[144,16]{1,0:T(8,128)} %get-tuple-element.22.pairs) | copy-start | bytes 27652
  65.2 0.7 copy-start.3
  65.9 20.8 %all-to-all-start.2 = ((bf16[32,16,256]{2,1,0:T(8,128)(2,1)}), bf16[32,16,256]{2,1,0:T(8,128)(2,1)S(1)}, u32[]{:S(2)}, u32[]{:S(2)}) async-start(bf16[32,16,256]{2,1,0:T(8,128)(2,1)} %bitcast.7), calls=%async_computation.2 | async-start | bytes 524288 | tf_op jit(solution)/shard_map/all_to_all | solution.py:406
